TPU v7x, 32 devices: a whole 2x2x4 slice. The times are simulated.
32 devices in a mesh: dp: 8 (over z, y), fsdp: 4 (over x, core).
Axes of the slice: x: 2, y: 2, z: 4, core: 2. Of those that a mesh axis runs over, the one named last changes fastest.
Arguments:
- tokens: bfloat16 [16384, 768], P(('dp', 'fsdp')), may hold values from -6 to 6
- cotangent: bfloat16 [16384, 768], P(('dp', 'fsdp')), may hold values from -6 to 6
- segment_ids: int32 [16384], P('dp'), may hold values from 0 to 24, as said below
- segment_starts: int32 [16384], P('dp'), may hold values from 0 to 2047, as said below
- padding_mask: int32 [16384], P('dp'), may hold values from 0 to 1, as said below
- lead_index: int32 [8], P('dp'), may hold values from 0 to 19
- input_weights: float32 [2, 768, 2304], P(None, ('dp', 'fsdp')), may hold values from -0.21875 to 0.21875
- input_moment: float32 [2, 768, 2304], P(None, ('dp', 'fsdp')), may hold values from -224 to 224
- input_square: float32 [2, 768, 2304], P(None, ('dp', 'fsdp')), may hold values from 737.28 to 11796.48
- output_weights: float32 [2, 768, 768], P(None, ('dp', 'fsdp')), may hold values from -0.875 to 0.875
- output_moment: float32 [2, 768, 768], P(None, ('dp', 'fsdp')), may hold values from -160 to 160
- output_square: float32 [2, 768, 768], P(None, ('dp', 'fsdp')), may hold values from 327.68 to 5242.88
- expand_weights: float32 [2, 768, 3072], P(None, ('dp', 'fsdp')), may hold values from -0.21875 to 0.21875
- expand_moment: float32 [2, 768, 3072], P(None, ('dp', 'fsdp')), may hold values from -192 to 192
- expand_square: float32 [2, 768, 3072], P(None, ('dp', 'fsdp')), may hold values from 491.52 to 8192
- shrink_weights: float32 [2, 3072, 768], P(None, ('dp', 'fsdp')), may hold values from -0.109375 to 0.109375
- shrink_moment: float32 [2, 3072, 768], P(None, ('dp', 'fsdp')), may hold values from -448 to 448
- shrink_square: float32 [2, 3072, 768], P(None, ('dp', 'fsdp')), may hold values from 2949.12 to 47185.92
- bias_vector: float32 [2, 9, 768], P(None, None, ('dp', 'fsdp')), may hold values from -4 to 4
- bias_moment: float32 [2, 9, 768], P(None, None, ('dp', 'fsdp')), may hold values from -384 to 384
- bias_square: float32 [2, 9, 768], P(None, None, ('dp', 'fsdp')), may hold values from 2048 to 32768
- lead_table: float32 [2, 20, 3072], P(None, None, ('dp', 'fsdp')), may hold values from -4 to 4
- lead_moment: float32 [2, 20, 3072], P(None, None, ('dp', 'fsdp')), may hold values from -80 to 80
- lead_square: float32 [2, 20, 3072], P(None, None, ('dp', 'fsdp')), may hold values from 102.375 to 1638
Outputs:
- out_tokens: float32 [16384, 768], P(('dp', 'fsdp'))
- in_grad: float32 [16384, 768], P(('dp', 'fsdp'))
- input_updated: float32 [2, 768, 2304], P(None, ('dp', 'fsdp'))
- input_moments: float32 [2, 768, 2304], P(None, ('dp', 'fsdp'))
- input_squares: float32 [2, 768, 2304], P(None, ('dp', 'fsdp'))
- input_copies: bfloat16 [2, 768, 2304], P(None, ('dp', 'fsdp'))
- output_updated: float32 [2, 768, 768], P(None, ('dp', 'fsdp'))
- output_moments: float32 [2, 768, 768], P(None, ('dp', 'fsdp'))
- output_squares: float32 [2, 768, 768], P(None, ('dp', 'fsdp'))
- output_copies: bfloat16 [2, 768, 768], P(None, ('dp', 'fsdp'))
- expand_updated: float32 [2, 768, 3072], P(None, ('dp', 'fsdp'))
- expand_moments: float32 [2, 768, 3072], P(None, ('dp', 'fsdp'))
- expand_squares: float32 [2, 768, 3072], P(None, ('dp', 'fsdp'))
- expand_copies: bfloat16 [2, 768, 3072], P(None, ('dp', 'fsdp'))
- shrink_updated: float32 [2, 3072, 768], P(None, ('dp', 'fsdp'))
- shrink_moments: float32 [2, 3072, 768], P(None, ('dp', 'fsdp'))
- shrink_squares: float32 [2, 3072, 768], P(None, ('dp', 'fsdp'))
- shrink_copies: bfloat16 [2, 3072, 768], P(None, ('dp', 'fsdp'))
- bias_updated: float32 [2, 9, 768], P(None, None, ('dp', 'fsdp'))
- bias_moments: float32 [2, 9, 768], P(None, None, ('dp', 'fsdp'))
- bias_squares: float32 [2, 9, 768], P(None, None, ('dp', 'fsdp'))
- bias_copies: bfloat16 [2, 9, 768], P(None, None, ('dp', 'fsdp'))
- lead_updated: float32 [2, 20, 3072], P(None, None, ('dp', 'fsdp'))
- lead_moments: float32 [2, 20, 3072], P(None, None, ('dp', 'fsdp'))
- lead_squares: float32 [2, 20, 3072], P(None, None, ('dp', 'fsdp'))
- lead_copies: bfloat16 [2, 20, 3072], P(None, None, ('dp', 'fsdp'))
Inputs may be any that keep to these rules, and one draw needn't show every extreme that they name: `segment_ids`: in each sequence of 2048 patches the window number starts at 0 and rises by one at each new window; every window but a sequence's last holds 64 to 512 consecutive patches, and some window of every sequence holds exactly 512; the last one may be cut by the sequence's end. `segment_starts`: equal for all patches of one window: the position of its first patch within the sequence. `padding_mask`: 0 exactly on the patches of a sequence's last window where it is cut by the sequence's end.
All inputs are finite; a program needn't handle non-finite values.
Results may differ from a plain program's by a relative error of at most 0.015.
Values may be sent and summed in bfloat16 or wider, within the bound.
A program may use at most 384 MiB of HBM per device.

v0:
```python
import math

import jax
import jax.numpy as jnp
from jax import lax
from jax.sharding import PartitionSpec as P

D = 768
FF = 3072
HEADS = 12
HEAD_DIM = 64
LEADS = 20
LAYERS = 2
WIN_MAX = 512
STEP = 10


EPSILON = 1e-06
NEGATIVE = -1e30
BETA_ONE = 0.5
BETA_TWO = 0.5
RATE_MATRIX = 0.08
RATE_VECTOR = 0.3
DECAY = 0.1
ADAM_EPSILON = 1e-08


def with_halo(cells, sides, width):
    for axis, dim in sides:
        count = lax.axis_size(axis)
        ends = count - 1
        head = lax.slice_in_dim(cells, 0, width, axis=dim)
        tail = lax.slice_in_dim(cells, cells.shape[dim] - width, cells.shape[dim], axis=dim)
        cells = jnp.concatenate(
            [
                lax.ppermute(tail, axis, [(i, (i + 1) % count) for i in range(ends)]),
                cells,
                lax.ppermute(head, axis, [((i + 1) % count, i) for i in range(ends)]),
            ],
            axis=dim,
        )
    return cells


def passed_along(value, axis, by):
    size = lax.axis_size(axis)
    pairs = [(i, i + by) for i in range(size) if 0 <= i + by < size]
    return lax.ppermute(value, axis, pairs)


def normalize(values):
    centred = values - jnp.mean(values, axis=-1, keepdims=True)
    inverse = lax.rsqrt(jnp.mean(centred * centred, axis=-1, keepdims=True) + EPSILON)
    return (centred * inverse, inverse)


def normalize_back(grad_normed, normed, inverse):
    return inverse * (
        grad_normed
        - jnp.mean(grad_normed, axis=-1, keepdims=True)
        - normed * jnp.mean(grad_normed * normed, axis=-1, keepdims=True)
    )


def rotary_tables(relative):
    indices = jnp.arange(HEAD_DIM // 2).astype(jnp.float32)
    frequency = jnp.exp(indices * (-2.0 * math.log(10000.0) / HEAD_DIM))
    phase = relative.astype(jnp.float32)[:, None] * frequency[None, :]
    return (jnp.cos(phase)[:, None, :], jnp.sin(phase)[:, None, :])


def rotate(field, cosine_table, sine_table):
    half_dim = field.shape[-1] // 2
    first_half = field[..., :half_dim]
    second = field[..., half_dim:]
    return jnp.concatenate(
        [
            first_half * cosine_table - second * sine_table,
            second * cosine_table + first_half * sine_table,
        ],
        axis=-1,
    )


def rotate_back(field, cosine_table, sine_table):
    half_dim = field.shape[-1] // 2
    first_half = field[..., :half_dim]
    second = field[..., half_dim:]
    return jnp.concatenate(
        [
            first_half * cosine_table + second * sine_table,
            second * cosine_table - first_half * sine_table,
        ],
        axis=-1,
    )


def fetch_layer(masters, layer_index):
    first_matrix = masters[0][layer_index].astype(jnp.bfloat16)
    second_matrix = masters[1][layer_index].astype(jnp.bfloat16)
    third_matrix = masters[2][layer_index].astype(jnp.bfloat16)
    fourth_matrix = masters[3][layer_index].astype(jnp.bfloat16)
    bias_part = masters[4][layer_index].astype(jnp.bfloat16)
    table_part = jnp.transpose(masters[5][layer_index].astype(jnp.bfloat16))
    whole = (
        lax.all_gather(first_matrix, ("dp", "fsdp"), axis=0, tiled=True),
        lax.all_gather(second_matrix, ("dp", "fsdp"), axis=0, tiled=True),
        lax.all_gather(third_matrix, ("dp", "fsdp"), axis=0, tiled=True),
        lax.all_gather(fourth_matrix, ("dp", "fsdp"), axis=0, tiled=True),
        lax.all_gather(bias_part, ("dp", "fsdp"), axis=1, tiled=True),
        lax.all_gather(table_part, ("dp", "fsdp"), axis=0, tiled=True),
    )
    return (whole[0], whole[1], whole[2], whole[3], whole[4], jnp.transpose(whole[5]))


def reduce_layer(gradients):
    grad_first, grad_second, grad_third, grad_fourth, grad_bias, grad_table = gradients
    table_turned = jnp.transpose(grad_table)
    summed = (
        lax.psum_scatter(grad_first, ("dp", "fsdp"), scatter_dimension=0, tiled=True),
        lax.psum_scatter(grad_second, ("dp", "fsdp"), scatter_dimension=0, tiled=True),
        lax.psum_scatter(grad_third, ("dp", "fsdp"), scatter_dimension=0, tiled=True),
        lax.psum_scatter(grad_fourth, ("dp", "fsdp"), scatter_dimension=0, tiled=True),
        lax.psum_scatter(grad_bias, ("dp", "fsdp"), scatter_dimension=1, tiled=True),
        lax.psum_scatter(table_turned, ("dp", "fsdp"), scatter_dimension=0, tiled=True),
    )
    return (summed[0], summed[1], summed[2], summed[3], summed[4], jnp.transpose(summed[5]))


def build_masks(segment_ids, padding_mask, offset, row_count):
    block_size = min(512, row_count)
    band_size = block_size + 2 * WIN_MAX
    filler = jnp.full((WIN_MAX,), -1, jnp.int32)
    nothing = jnp.zeros((WIN_MAX,), jnp.int32)
    segment_wide = lax.dynamic_slice_in_dim(
        jnp.concatenate([filler, segment_ids, filler]), offset, row_count + 2 * WIN_MAX
    )
    live_wide = lax.dynamic_slice_in_dim(
        jnp.concatenate([nothing, padding_mask, nothing]), offset, row_count + 2 * WIN_MAX
    )
    segment_own = lax.dynamic_slice_in_dim(segment_ids, offset, row_count)
    diagonal = jnp.arange(block_size)[:, None] + WIN_MAX == jnp.arange(band_size)[None, :]
    block_masks = [
        (segment_own[:, None] == segment_wide[None, :]) & (live_wide[None, :] == 1) | diagonal
    ]
    return block_masks


def block_scores(query_block, key_block, allowed):
    raw_scores = jnp.einsum(
        "qhd,khd->hqk", query_block, key_block, preferred_element_type=jnp.float32
    ) * HEAD_DIM ** (-0.5)
    return jnp.where(allowed[None, :, :], raw_scores, NEGATIVE)


def attend_forward(queries, extended, block_masks):
    block_size = block_masks[0].shape[0]
    band_size = block_masks[0].shape[1]
    outputs = []
    log_totals = []
    for block_index, allowed in enumerate(block_masks):
        low_edge = block_index * block_size
        key_block = extended[low_edge : low_edge + band_size, :D].reshape(
            band_size, HEADS, HEAD_DIM
        )
        value_block = extended[low_edge : low_edge + band_size, D:].reshape(
            band_size, HEADS, HEAD_DIM
        )
        masked = block_scores(queries, key_block, allowed)
        row_peak = jnp.max(masked, axis=-1, keepdims=True)
        log_total = row_peak + jnp.log(jnp.sum(jnp.exp(masked - row_peak), axis=-1, keepdims=True))
        weights = jnp.exp(masked - log_total).astype(jnp.bfloat16)
        outputs.append(
            jnp.einsum("hqk,khd->qhd", weights, value_block, preferred_element_type=jnp.float32)
        )
        log_totals.append(log_total)
    return (outputs[0], log_totals)


def attend_backward(queries, extended, log_totals, grad_attended, block_masks):
    block_size = block_masks[0].shape[0]
    band_size = block_masks[0].shape[1]
    grad_queries = []
    grad_extended = jnp.zeros((extended.shape[0], 2 * D), jnp.float32)
    for block_index, allowed in enumerate(block_masks):
        low_edge = block_index * block_size
        key_block = extended[low_edge : low_edge + band_size, :D].reshape(
            band_size, HEADS, HEAD_DIM
        )
        value_block = extended[low_edge : low_edge + band_size, D:].reshape(
            band_size, HEADS, HEAD_DIM
        )
        masked = block_scores(queries, key_block, allowed)
        probabilities = jnp.exp(masked - log_totals[block_index])
        weights = probabilities.astype(jnp.bfloat16)
        grad_weights = jnp.einsum(
            "qhd,khd->hqk", grad_attended, value_block, preferred_element_type=jnp.float32
        )
        row_delta = jnp.sum(probabilities * grad_weights, axis=-1, keepdims=True)
        grad_scores = (probabilities * (grad_weights - row_delta)).astype(jnp.bfloat16)
        grad_queries.append(
            jnp.einsum("hqk,khd->qhd", grad_scores, key_block, preferred_element_type=jnp.float32)
            * HEAD_DIM ** (-0.5)
        )
        grad_keys = jnp.einsum(
            "hqk,qhd->khd", grad_scores, queries, preferred_element_type=jnp.float32
        ) * HEAD_DIM ** (-0.5)
        grad_values = jnp.einsum(
            "hqk,qhd->khd", weights, grad_attended, preferred_element_type=jnp.float32
        )
        grad_extended = grad_extended.at[low_edge : low_edge + band_size].add(
            jnp.concatenate(
                [grad_keys.reshape(band_size, D), grad_values.reshape(band_size, D)], axis=1
            )
        )
    return (grad_queries[0], grad_extended)


def forward_layer(stream, gathered, context):
    in_full, out_full, expand_full, shrink_full, bias_full, table_full = gathered
    cosine_table, sine_table, block_masks, lead_row, lead_hot = context
    biases = bias_full.astype(jnp.float32).reshape(-1)
    modulation = lax.dynamic_index_in_dim(table_full, lead_row, 0, keepdims=False).astype(
        jnp.float32
    )
    shift_one = modulation[:D]
    scale_one = modulation[D : 2 * D]
    shift_two = modulation[2 * D : 3 * D]
    scale_two = modulation[3 * D :]
    normed_one, inverse_one = normalize(stream)
    input_one = (normed_one * (1.0 + scale_one) + shift_one).astype(jnp.bfloat16)
    projected = jnp.dot(input_one, in_full, preferred_element_type=jnp.float32) + biases[: 3 * D]
    queries = rotate(
        projected[:, :D].reshape(-1, HEADS, HEAD_DIM), cosine_table, sine_table
    ).astype(jnp.bfloat16)
    rotated_keys = rotate(
        projected[:, D : 2 * D].reshape(-1, HEADS, HEAD_DIM), cosine_table, sine_table
    ).astype(jnp.bfloat16)
    values = projected[:, 2 * D :].astype(jnp.bfloat16)
    extended = with_halo(
        jnp.concatenate([rotated_keys.reshape(-1, D), values], axis=1), (("fsdp", 0),), WIN_MAX
    )
    attended, log_totals = attend_forward(queries, extended, block_masks)
    attended = attended.reshape(-1, D).astype(jnp.bfloat16)
    middle = stream + (
        jnp.dot(attended, out_full, preferred_element_type=jnp.float32) + biases[3 * D : 4 * D]
    )
    normed_two, inverse_two = normalize(middle)
    input_two = (normed_two * (1.0 + scale_two) + shift_two).astype(jnp.bfloat16)
    hidden = (
        jnp.dot(input_two, expand_full, preferred_element_type=jnp.float32)
        + biases[4 * D : 4 * D + FF]
    )
    active = jax.nn.gelu(hidden, approximate=False).astype(jnp.bfloat16)
    result = middle + (
        jnp.dot(active, shrink_full, preferred_element_type=jnp.float32) + biases[4 * D + FF :]
    )
    saved_values = (
        normed_one,
        inverse_one,
        input_one,
        queries,
        extended,
        log_totals,
        attended,
        normed_two,
        inverse_two,
        input_two,
        hidden,
        active,
        modulation,
    )
    return (result, saved_values)


def backward_layer(grad_stream, gathered, saved_values, context):
    in_full, out_full, expand_full, shrink_full, bias_full, table_full = gathered
    cosine_table, sine_table, block_masks, lead_row, lead_hot = context
    (
        normed_one,
        inverse_one,
        input_one,
        queries,
        extended,
        log_totals,
        attended,
        normed_two,
        inverse_two,
        input_two,
        hidden,
        active,
        modulation,
    ) = saved_values
    row_count = grad_stream.shape[0]
    scale_one = modulation[D : 2 * D]
    scale_two = modulation[3 * D :]
    grad_low = grad_stream.astype(jnp.bfloat16)
    grad_shrink = jnp.einsum("tf,td->fd", active, grad_low, preferred_element_type=jnp.float32)
    bias_shrink = jnp.sum(grad_low.astype(jnp.float32), axis=0)
    grad_active = jnp.einsum("td,fd->tf", grad_low, shrink_full, preferred_element_type=jnp.float32)
    gelu_value, gelu_pull = jax.vjp(
        lambda hidden_in: jax.nn.gelu(hidden_in, approximate=False), hidden
    )
    grad_hidden = gelu_pull(grad_active)[0].astype(jnp.bfloat16)
    grad_expand = jnp.einsum(
        "tc,tf->cf", input_two, grad_hidden, preferred_element_type=jnp.float32
    )
    bias_expand = jnp.sum(grad_hidden.astype(jnp.float32), axis=0)
    grad_input_two = jnp.einsum(
        "tf,cf->tc", grad_hidden, expand_full, preferred_element_type=jnp.float32
    )
    shift_two_grad = jnp.sum(grad_input_two, axis=0)
    scale_two_grad = jnp.sum(grad_input_two * normed_two, axis=0)
    grad_middle = grad_stream + normalize_back(
        grad_input_two * (1.0 + scale_two), normed_two, inverse_two
    )
    middle_low = grad_middle.astype(jnp.bfloat16)
    grad_output = jnp.einsum("te,td->ed", attended, middle_low, preferred_element_type=jnp.float32)
    bias_output = jnp.sum(middle_low.astype(jnp.float32), axis=0)
    grad_attended = jnp.einsum(
        "td,ed->te", middle_low, out_full, preferred_element_type=jnp.float32
    )
    grad_attended = grad_attended.astype(jnp.bfloat16).reshape(row_count, HEADS, HEAD_DIM)
    grad_queries, grad_extended = attend_backward(
        queries, extended, log_totals, grad_attended, block_masks
    )
    lower_rim = grad_extended[:WIN_MAX]
    upper_rim = grad_extended[WIN_MAX + row_count :]
    from_above = passed_along(lower_rim.astype(jnp.bfloat16), "fsdp", -1).astype(lower_rim.dtype)
    from_below = passed_along(upper_rim.astype(jnp.bfloat16), "fsdp", 1).astype(upper_rim.dtype)
    own_rows = grad_extended[WIN_MAX : WIN_MAX + row_count]
    own_rows = own_rows.at[:WIN_MAX].add(from_below)
    own_rows = own_rows.at[row_count - WIN_MAX :].add(from_above)
    grad_query_pre = rotate_back(grad_queries, cosine_table, sine_table).reshape(row_count, D)
    grad_key_pre = rotate_back(
        own_rows[:, :D].reshape(row_count, HEADS, HEAD_DIM), cosine_table, sine_table
    ).reshape(row_count, D)
    grad_projected = jnp.concatenate(
        [grad_query_pre, grad_key_pre, own_rows[:, D:]], axis=1
    ).astype(jnp.bfloat16)
    grad_input = jnp.einsum(
        "tc,te->ce", input_one, grad_projected, preferred_element_type=jnp.float32
    )
    bias_input = jnp.sum(grad_projected.astype(jnp.float32), axis=0)
    grad_input_one = jnp.einsum(
        "te,ce->tc", grad_projected, in_full, preferred_element_type=jnp.float32
    )
    shift_one_grad = jnp.sum(grad_input_one, axis=0)
    scale_one_grad = jnp.sum(grad_input_one * normed_one, axis=0)
    grad_before = grad_middle + normalize_back(
        grad_input_one * (1.0 + scale_one), normed_one, inverse_one
    )
    grad_bias = jnp.concatenate([bias_input, bias_output, bias_expand, bias_shrink]).reshape(-1, D)
    grad_table = (
        lead_hot[:, None]
        * jnp.concatenate([shift_one_grad, scale_one_grad, shift_two_grad, scale_two_grad])[None, :]
    )
    return (grad_before, (grad_input, grad_output, grad_expand, grad_shrink, grad_bias, grad_table))


def adam_update(weight, gradient, moment, square, step_rate, decay_rate):
    moment = BETA_ONE * moment + (1.0 - BETA_ONE) * gradient
    square = BETA_TWO * square + (1.0 - BETA_TWO) * gradient * gradient
    first_fix = 1.0 - BETA_ONE**STEP
    second_fix = 1.0 - BETA_TWO**STEP
    update = moment / first_fix / (jnp.sqrt(square / second_fix) + ADAM_EPSILON)
    weight = weight - step_rate * (update + decay_rate * weight)
    return (weight, moment, square, weight.astype(jnp.bfloat16))


def shards(
    tokens,
    cotangent,
    segment_ids,
    segment_starts,
    padding_mask,
    lead_index,
    input_weights,
    input_moment,
    input_square,
    output_weights,
    output_moment,
    output_square,
    expand_weights,
    expand_moment,
    expand_square,
    shrink_weights,
    shrink_moment,
    shrink_square,
    bias_vector,
    bias_moment,
    bias_square,
    lead_table,
    lead_moment,
    lead_square,
):
    row_count = tokens.shape[0]
    offset = lax.axis_index("fsdp") * row_count
    block_masks = build_masks(segment_ids, padding_mask, offset, row_count)
    own_starts = lax.dynamic_slice_in_dim(segment_starts, offset, row_count)
    relative = offset + jnp.arange(row_count, dtype=jnp.int32) - own_starts
    cosine_table, sine_table = rotary_tables(relative)
    lead_row = lead_index[0]
    lead_hot = (jnp.arange(LEADS, dtype=jnp.int32) == lead_row).astype(jnp.float32)
    context = (cosine_table, sine_table, block_masks, lead_row, lead_hot)
    masters = (
        input_weights,
        output_weights,
        expand_weights,
        shrink_weights,
        bias_vector,
        lead_table,
    )
    stream = tokens.astype(jnp.float32)
    gathered_layers = []
    saved_layers = []
    for layer_index in range(LAYERS):
        gathered = fetch_layer(masters, layer_index)
        stream, saved_values = forward_layer(stream, gathered, context)
        gathered_layers.append(gathered)
        saved_layers.append(saved_values)
    grad_stream = cotangent.astype(jnp.float32)
    reduced_layers = [None] * LAYERS
    for layer_index in reversed(range(LAYERS)):
        gathered = fetch_layer(masters, layer_index)
        grad_stream, layer_grads = backward_layer(
            grad_stream, gathered, saved_layers[layer_index], context
        )
        reduced_layers[layer_index] = reduce_layer(layer_grads)
    moments = (input_moment, output_moment, expand_moment, shrink_moment, bias_moment, lead_moment)
    squares = (input_square, output_square, expand_square, shrink_square, bias_square, lead_square)
    results = []
    for number in range(6):
        stacked = jnp.stack([reduced_layers[layer_index][number] for layer_index in range(LAYERS)])
        step_rate = RATE_MATRIX if number < 4 else RATE_VECTOR
        decay_rate = DECAY if number < 4 else 0.0
        results.append(
            adam_update(
                masters[number], stacked, moments[number], squares[number], step_rate, decay_rate
            )
        )
    return (
        stream,
        grad_stream,
        results[0][0],
        results[0][1],
        results[0][2],
        results[0][3],
        results[1][0],
        results[1][1],
        results[1][2],
        results[1][3],
        results[2][0],
        results[2][1],
        results[2][2],
        results[2][3],
        results[3][0],
        results[3][1],
        results[3][2],
        results[3][3],
        results[4][0],
        results[4][1],
        results[4][2],
        results[4][3],
        results[5][0],
        results[5][1],
        results[5][2],
        results[5][3],
    )


def solution(mesh):
    return jax.shard_map(
        shards,
        mesh=mesh,
        in_specs=(
            P(("dp", "fsdp"), None),
            P(("dp", "fsdp"), None),
            P("dp"),
            P("dp"),
            P("dp"),
            P("dp"),
            P(None, ("dp", "fsdp"), None),
            P(None, ("dp", "fsdp"), None),
            P(None, ("dp", "fsdp"), None),
            P(None, ("dp", "fsdp"), None),
            P(None, ("dp", "fsdp"), None),
            P(None, ("dp", "fsdp"), None),
            P(None, ("dp", "fsdp"), None),
            P(None, ("dp", "fsdp"), None),
            P(None, ("dp", "fsdp"), None),
            P(None, ("dp", "fsdp"), None),
            P(None, ("dp", "fsdp"), None),
            P(None, ("dp", "fsdp"), None),
            P(None, None, ("dp", "fsdp")),
            P(None, None, ("dp", "fsdp")),
            P(None, None, ("dp", "fsdp")),
            P(None, None, ("dp", "fsdp")),
            P(None, None, ("dp", "fsdp")),
            P(None, None, ("dp", "fsdp")),
        ),
        out_specs=(
            P(("dp", "fsdp"), None),
            P(("dp", "fsdp"), None),
            P(None, ("dp", "fsdp"), None),
            P(None, ("dp", "fsdp"), None),
            P(None, ("dp", "fsdp"), None),
            P(None, ("dp", "fsdp"), None),
            P(None, ("dp", "fsdp"), None),
            P(None, ("dp", "fsdp"), None),
            P(None, ("dp", "fsdp"), None),
            P(None, ("dp", "fsdp"), None),
            P(None, ("dp", "fsdp"), None),
            P(None, ("dp", "fsdp"), None),
            P(None, ("dp", "fsdp"), None),
            P(None, ("dp", "fsdp"), None),
            P(None, ("dp", "fsdp"), None),
            P(None, ("dp", "fsdp"), None),
            P(None, ("dp", "fsdp"), None),
            P(None, ("dp", "fsdp"), None),
            P(None, None, ("dp", "fsdp")),
            P(None, None, ("dp", "fsdp")),
            P(None, None, ("dp", "fsdp")),
            P(None, None, ("dp", "fsdp")),
            P(None, None, ("dp", "fsdp")),
            P(None, None, ("dp", "fsdp")),
            P(None, None, ("dp", "fsdp")),
            P(None, None, ("dp", "fsdp")),
        ),
        check_vma=False,
    )
```

profile of v0, /device:TPU:0, one launch (start us, length us, event | category | flops | bytes accessed | tf_op | source)
XLA Modules:
  0.0 2029.9 jit_solution(13256587539186870728)
XLA Ops:
  17.2 44.0 %all-gather.11 = bf16[32,96,20]{1,2,0:T(8,128)(2,1)S(1)} all-gather(bf16[1,96,20]{1,2,0:T(8,128)(2,1)S(1)} %get-tuple-element.333), channel_id=1, replica_groups=mesh['dp'=8,'fsdp'=4] {'dp','fsdp'}, dimensions={0}, use_global_device_ids=true | all-gather | bytes 126720 | tf_op jit(solution)/shard_map/all_gather | solution.py:111
  61.4 37.3 %all-gather.10 = bf16[32,96,20]{1,2,0:T(8,128)(2,1)S(1)} all-gather(bf16[1,96,20]{1,2,0:T(8,128)(2,1)S(1)} %get-tuple-element.334), channel_id=1, replica_groups=mesh['dp'=8,'fsdp'=4] {'dp','fsdp'}, dimensions={0}, use_global_device_ids=true | all-gather | bytes 126720 | tf_op jit(solution)/shard_map/all_gather | solution.py:111
  100.2 39.3 %all-gather.1 = bf16[1,9,768]{1,0,2:T(2,128)(2,1)S(1)} all-gather(bf16[1,9,24]{1,0,2:T(2,128)(2,1)S(1)} %get-tuple-element.336), channel_id=3, replica_groups=mesh['dp'=8,'fsdp'=4] {'dp','fsdp'}, dimensions={2}, use_global_device_ids=true | all-gather | bytes 14256 | tf_op jit(solution)/shard_map/all_gather | solution.py:110
  168.2 49.2 %all-gather.6 = bf16[1,9,768]{1,0,2:T(2,128)(2,1)S(1)} all-gather(bf16[1,9,24]{1,0,2:T(2,128)(2,1)S(1)} %get-tuple-element.335), channel_id=8, replica_groups=mesh['dp'=8,'fsdp'=4] {'dp','fsdp'}, dimensions={2}, use_global_device_ids=true | all-gather | bytes 14256 | tf_op jit(solution)/shard_map/all_gather | solution.py:110
  297.6 20.1 multiply_convert_fusion.3
  426.3 26.8 %all-gather.33.cloned.1.call-done = bf16[1,768,3072]{2,1,0:T(8,128)(2,1)} async-done(((bf16[1,24,3072]{2,1,0:T(8,128)(2,1)}), bf16[1,768,3072]{2,1,0:T(8,128)(2,1)}) %all-gather.33.cloned.1.call-update) | async-done | bytes 4718608 | tf_op jit(solution)/shard_map/all_gather | solution.py:108
  453.1 19.7 multiply_convert_fusion.2
  472.9 46.2 %all-gather.35.cloned.1.call-done = bf16[1,3072,768]{2,1,0:T(8,128)(2,1)} async-done(((bf16[1,96,768]{2,1,0:T(8,128)(2,1)}), bf16[1,3072,768]{2,1,0:T(8,128)(2,1)}) %all-gather.35.cloned.1.call-update) | async-done | bytes 4718608 | tf_op jit(solution)/shard_map/all_gather | solution.py:109
  538.0 18.1 fusion.79
  556.1 28.3 %multiply_reduce_fusion.1 = (f32[12,512]{1,0:T(8,128)S(1)}, f32[12,512,1536]{2,1,0:T(8,128)}) fusion(f32[12,512,1536]{2,1,0:T(8,128)} %get-tuple-element.349, f32[12,512]{1,0:T(8,128)S(1)} %log_add_fusion, pred[512,1536]{1,0:T(8,128)(4,1)S(1)} %fusion.46, bf16[512,12,64]{0,2,1:T(8,128)(2,1)S(1)} %bitcast.210, bf16[1536,12,64]{0,2,1:T(8,128)(2,1)} %bitcast.202), kind=kOutput, calls=%fused_computation.3 | convolution fusion | flops 1255139328 | bytes 79478784 | tf_op jit(solution)/shard_map/qhd,khd->hqk/dot_general | solution.py:196
  584.3 24.5 %multiply_convert_fusion.1 = bf16[12,512,1536]{2,1,0:T(8,128)(2,1)S(1)} fusion(f32[12,512,1536]{2,1,0:T(8,128)} %get-tuple-element.355, f32[12,512,1536]{2,1,0:T(8,128)} %get-tuple-element.349, f32[12,512]{1,0:T(8,128)S(1)} %get-tuple-element.354, f32[12,512]{1,0:T(8,128)S(1)} %log_add_fusion, pred[512,1536]{1,0:T(8,128)(4,1)S(1)} %fusion.46), kind=kLoop, calls=%fused_computation.2 | loop fusion | flops 56623104 | bytes 95207424 | tf_op jit(solution)/shard_map/convert_element_type | solution.py:200
  670.1 18.2 fusion.82
  688.3 28.2 %multiply_reduce_fusion = (f32[12,512]{1,0:T(8,128)S(1)}, f32[12,512,1536]{2,1,0:T(8,128)}) fusion(f32[12,512,1536]{2,1,0:T(8,128)} %get-tuple-element.342, f32[12,512]{1,0:T(8,128)S(1)} %copy-done.56, pred[512,1536]{1,0:T(8,128)(4,1)S(1)} %fusion.46, bf16[512,12,64]{0,2,1:T(8,128)(2,1)S(1)} %bitcast.212, bf16[1536,12,64]{0,2,1:T(8,128)(2,1)} %bitcast.199), kind=kOutput, calls=%fused_computation.1 | convolution fusion | flops 1255139328 | bytes 79478784 | tf_op jit(solution)/shard_map/qhd,khd->hqk/dot_general | solution.py:196
  716.6 24.4 %multiply_convert_fusion = bf16[12,512,1536]{2,1,0:T(8,128)(2,1)S(1)} fusion(f32[12,512,1536]{2,1,0:T(8,128)} %get-tuple-element.359, f32[12,512,1536]{2,1,0:T(8,128)} %get-tuple-element.342, f32[12,512]{1,0:T(8,128)S(1)} %get-tuple-element.358, f32[12,512]{1,0:T(8,128)S(1)} %copy-done.57, pred[512,1536]{1,0:T(8,128)(4,1)S(1)} %fusion.46), kind=kLoop, calls=%fused_computation | loop fusion | flops 56623104 | bytes 95207424 | tf_op jit(solution)/shard_map/convert_element_type | solution.py:200
  865.3 49.4 %all-reduce.2 = (f32[9,768]{1,0:T(8,128)S(1)}, f32[9,768]{1,0:T(8,128)S(1)}) all-reduce(f32[9,768]{1,0:T(8,128)S(1)} %reshape.600, f32[9,768]{1,0:T(8,128)S(1)} %reshape.599), channel_id=21, replica_groups=mesh['dp'=8,'fsdp'=4] {'dp','fsdp'}, use_global_device_ids=true, to_apply=%region_39.40.clone | all-reduce | flops 13824 | bytes 110592
  921.6 78.2 %reduce-scatter.35.cloned.1.call-done = f32[96,20]{1,0:T(8,128)} async-done(((f32[3072,20]{1,0:T(8,128)}), f32[96,20]{1,0:T(8,128)}) %reduce-scatter.35.cloned.1.call-update) | async-done | bytes 7696
  1003.3 100.0 %reduce-scatter.23.cloned.1.call-done = f32[24,768]{1,0:T(8,128)} async-done(((f32[768,768]{1,0:T(8,128)}), f32[24,768]{1,0:T(8,128)}) %reduce-scatter.23.cloned.1.call-update) | async-done | bytes 73744 | tf_op jit(solution)/shard_map/reduce_scatter | solution.py:121
  1103.3 104.2 %reduce-scatter.21.cloned.1.call-done = f32[24,768]{1,0:T(8,128)} async-done(((f32[768,768]{1,0:T(8,128)}), f32[24,768]{1,0:T(8,128)}) %reduce-scatter.21.cloned.1.call-update) | async-done | bytes 73744 | tf_op jit(solution)/shard_map/reduce_scatter | solution.py:121
  1209.3 122.0 %reduce-scatter.19.cloned.1.call-done = f32[24,2304]{1,0:T(8,128)} async-done(((f32[768,2304]{1,0:T(8,128)}), f32[24,2304]{1,0:T(8,128)}) %reduce-scatter.19.cloned.1.call-update) | async-done | bytes 221200 | tf_op jit(solution)/shard_map/reduce_scatter | solution.py:120
  1331.3 124.7 %reduce-scatter.17.cloned.1.call-done = f32[24,2304]{1,0:T(8,128)} async-done(((f32[768,2304]{1,0:T(8,128)}), f32[24,2304]{1,0:T(8,128)}) %reduce-scatter.17.cloned.1.call-update) | async-done | bytes 221200 | tf_op jit(solution)/shard_map/reduce_scatter | solution.py:120
  1458.8 137.5 %reduce-scatter.27.cloned.1.call-done = f32[24,3072]{1,0:T(8,128)} async-done(((f32[768,3072]{1,0:T(8,128)}), f32[24,3072]{1,0:T(8,128)}) %reduce-scatter.27.cloned.1.call-update) | async-done | bytes 294928 | tf_op jit(solution)/shard_map/reduce_scatter | solution.py:122
  1596.3 141.6 %reduce-scatter.25.cloned.1.call-done = f32[24,3072]{1,0:T(8,128)} async-done(((f32[768,3072]{1,0:T(8,128)}), f32[24,3072]{1,0:T(8,128)}) %reduce-scatter.25.cloned.1.call-update) | async-done | bytes 294928 | tf_op jit(solution)/shard_map/reduce_scatter | solution.py:122
  1740.5 137.6 %reduce-scatter.31.cloned.1.call-done = f32[96,768]{1,0:T(8,128)} async-done(((f32[3072,768]{1,0:T(8,128)}), f32[96,768]{1,0:T(8,128)}) %reduce-scatter.31.cloned.1.call-update) | async-done | bytes 294928 | tf_op jit(solution)/shard_map/reduce_scatter | solution.py:123
  1878.2 141.6 %reduce-scatter.29.cloned.1.call-done = f32[96,768]{1,0:T(8,128)} async-done(((f32[3072,768]{1,0:T(8,128)}), f32[96,768]{1,0:T(8,128)}) %reduce-scatter.29.cloned.1.call-update) | async-done | bytes 294928 | tf_op jit(solution)/shard_map/reduce_scatter | solution.py:123
  (502 shorter events, 451.5 us)
Async XLA Ops:
  7.2 134.2 %all-gather.21.cloned.1.call-start = ((), (), s32[]{:S(2)}) async-start(), calls=%async_computation.18 | async-start | bytes 3649536 | tf_op jit(solution)/shard_map/all_gather | solution.py:106
  9.1 285.5 %all-gather.23.cloned.1.call-start = ((), (), s32[]{:S(2)}) async-start(), calls=%async_computation.19 | async-start | bytes 1216512 | tf_op jit(solution)/shard_map/all_gather | solution.py:107
  10.7 286.8 %all-gather.25.cloned.1.call-start = ((), (), s32[]{:S(2)}) async-start(), calls=%async_computation.20 | async-start | bytes 4866048 | tf_op jit(solution)/shard_map/all_gather | solution.py:108
  12.6 305.1 %all-gather.27.cloned.1.call-start = ((), (), s32[]{:S(2)}) async-start(), calls=%async_computation.21 | async-start | bytes 4866048 | tf_op jit(solution)/shard_map/all_gather | solution.py:109
  14.6 316.0 %all-gather.29.cloned.1.call-start = ((), (), s32[]{:S(2)}) async-start(), calls=%async_computation.22 | async-start | bytes 3649536 | tf_op jit(solution)/shard_map/all_gather | solution.py:106
  15.1 407.9 %all-gather.31.cloned.1.call-start = ((), (), s32[]{:S(2)}) async-start(), calls=%async_computation.23 | async-start | bytes 1216512 | tf_op jit(solution)/shard_map/all_gather | solution.py:107
  15.7 437.4 %all-gather.33.cloned.1.call-start = ((), (), s32[]{:S(2)}) async-start(), calls=%async_computation.24 | async-start | bytes 4866048 | tf_op jit(solution)/shard_map/all_gather | solution.py:108
  159.0 70.2 %collective-permute-start.1 = (bf16[512,1536]{1,0:T(8,128)(2,1)}, bf16[512,1536]{1,0:T(8,128)(2,1)}, u32[]{:S(2)}, u32[]{:S(2)}) collective-permute-start(bf16[512,1536]{1,0:T(8,128)(2,1)} %pad_maximum_fusion.6), channel_id=1, source_target_pairs={{1,0},{2,1},{3,2},{5,4},{6,5},{7,6},{9,8},{10,9},{11,10},{13,12},{... | collective-permute-start | bytes 4718600 | tf_op jit(solution)/shard_map/ppermute | solution.py:38
  160.3 68.9 %collective-permute-start = (bf16[512,1536]{1,0:T(8,128)(2,1)}, bf16[512,1536]{1,0:T(8,128)(2,1)}, u32[]{:S(2)}, u32[]{:S(2)}) collective-permute-start(bf16[512,1536]{1,0:T(8,128)(2,1)} %pad_maximum_fusion.6), channel_id=1, source_target_pairs={{0,1},{1,2},{2,3},{4,5},{5,6},{6,7},{8,9},{9,10},{10,11},{12,13},{... | collective-permute-start | bytes 4718600 | tf_op jit(solution)/shard_map/ppermute | solution.py:36
  164.6 354.5 %all-gather.35.cloned.1.call-start = ((), (), s32[]{:S(2)}) async-start(), calls=%async_computation.25 | async-start | bytes 4866048 | tf_op jit(solution)/shard_map/all_gather | solution.py:109
  346.5 13.2 collective-permute-start.3
  352.1 568.5 %reduce-scatter.33.cloned.1.call-start = ((), (), s32[]{:S(2)}) async-start(), calls=%async_computation.26 | async-start | bytes 1622016
  622.8 15.9 collective-permute-start.4
  626.3 12.5 collective-permute-start.5
  756.5 24.0 %collective-permute-start.6 = (bf16[512,1536]{0,1:T(8,128)(2,1)}, bf16[512,1536]{0,1:T(8,128)(2,1)}, u32[]{:S(2)}, u32[]{:S(2)}) collective-permute-start(bf16[512,1536]{0,1:T(8,128)(2,1)} %get-tuple-element.288), channel_id=1, source_target_pairs={{0,1},{1,2},{2,3},{4,5},{5,6},{6,7},{8,9},{9,10},{10,11},{12,13},{... | collective-permute-start | bytes 4718600 | tf_op jit(solution)/shard_map/ppermute | solution.py:48
  794.1 205.8 %reduce-scatter.35.cloned.1.call-start = ((), (), s32[]{:S(2)}) async-start(), calls=%async_computation.27 | async-start | bytes 1622016
  795.8 307.5 %reduce-scatter.23.cloned.1.call-start = ((), (), s32[]{:S(2)}) async-start(), calls=%async_computation.13 | async-start | bytes 2433024 | tf_op jit(solution)/shard_map/reduce_scatter | solution.py:121
  799.2 408.2 %reduce-scatter.21.cloned.1.call-start = ((), (), s32[]{:S(2)}) async-start(), calls=%async_computation.12 | async-start | bytes 2433024 | tf_op jit(solution)/shard_map/reduce_scatter | solution.py:121
  802.7 528.6 %reduce-scatter.19.cloned.1.call-start = ((), (), s32[]{:S(2)}) async-start(), calls=%async_computation.11 | async-start | bytes 7299072 | tf_op jit(solution)/shard_map/reduce_scatter | solution.py:120
  809.8 646.2 %reduce-scatter.17.cloned.1.call-start = ((), (), s32[]{:S(2)}) async-start(), calls=%async_computation.10 | async-start | bytes 7299072 | tf_op jit(solution)/shard_map/reduce_scatter | solution.py:120
  817.8 778.5 %reduce-scatter.27.cloned.1.call-start = ((), (), s32[]{:S(2)}) async-start(), calls=%async_computation.15 | async-start | bytes 9732096 | tf_op jit(solution)/shard_map/reduce_scatter | solution.py:122
  826.4 911.4 %reduce-scatter.25.cloned.1.call-start = ((), (), s32[]{:S(2)}) async-start(), calls=%async_computation.14 | async-start | bytes 9732096 | tf_op jit(solution)/shard_map/reduce_scatter | solution.py:122
  835.0 1043.1 %reduce-scatter.31.cloned.1.call-start = ((), (), s32[]{:S(2)}) async-start(), calls=%async_computation.17 | async-start | bytes 9732096 | tf_op jit(solution)/shard_map/reduce_scatter | solution.py:123
  844.4 1175.4 %reduce-scatter.29.cloned.1.call-start = ((), (), s32[]{:S(2)}) async-start(), calls=%async_computation.16 | async-start | bytes 9732096 | tf_op jit(solution)/shard_map/reduce_scatter | solution.py:123
  (134 other events, 7883.2 us)
Sparse Core Ops, SparseCore 0:
  11.5 63.5 all-gather.20
  78.6 53.0 all-gather.22
  135.2 66.3 all-gather.24
  204.9 63.2 all-gather.26
  271.5 58.9 all-gather.28
  333.9 53.0 all-gather.30
  390.5 62.5 all-gather.32
  456.6 62.4 all-gather.34
  794.2 104.4 reduce-scatter.32
  903.8 96.0 reduce-scatter.34
  1005.2 98.0 reduce-scatter.22
  1109.3 98.1 reduce-scatter.20
  1213.1 118.1 reduce-scatter.18
  1337.8 118.1 reduce-scatter.16
  1461.7 134.5 reduce-scatter.26
  1603.1 134.7 reduce-scatter.24
  1743.6 134.5 reduce-scatter.30
  1884.9 134.7 reduce-scatter.28
where the time goes:
time: 2040 us; the launch traced here: 2030 us
  waiting for transfers between devices  1170 us (57%)
  matrix products  350 us (17%)
  blocking collectives  219 us (11%)
  other arithmetic  151 us (7%)
  local copies, waits for them, and re-layouts  93.2 us (5%)
  starting transfers between devices  31.6 us (2%)
    reduce_scatter x2, waiting for transfers between devices, reduce_layer(): lax.psum_scatter(grad_fourth, ('dp', 'fsdp'), scatter_dimension=0, tiled=...  279 us
    reduce_scatter x2, waiting for transfers between devices, reduce_layer(): lax.psum_scatter(grad_third, ('dp', 'fsdp'), scatter_dimension=0, tiled=T...  279 us
    reduce_scatter x2, waiting for transfers between devices, reduce_layer(): lax.psum_scatter(grad_first, ('dp', 'fsdp'), scatter_dimension=0, tiled=T...  247 us
    reduce_scatter x2, waiting for transfers between devices, reduce_layer(): lax.psum_scatter(grad_second, ('dp', 'fsdp'), scatter_dimension=0, tiled=...  204 us
    all_gather x2, blocking collectives, fetch_layer(): lax.all_gather(bias_part, ('dp', 'fsdp'), axis=1, tiled=True)  88.5 us
    all_gather x2, blocking collectives, fetch_layer(): lax.all_gather(table_part, ('dp', 'fsdp'), axis=0, tiled=True)  81.3 us
    unnamed x20, waiting for transfers between devices  79.6 us
    dot_general x2, matrix products, attend_backward(): jnp.einsum('qhd,khd->hqk', grad_attended, value_block, preferred_element_...  56.5 us
  transfers between devices with their start and end apart: 26, of which 12 were waited for; matrix products, arithmetic and copies ran while one was open for 17% of the time, Pallas kernels for 0%

commit v1 on v0

--- a/solution.py
+++ b/solution.py
@@ -1,8 +1,11 @@
+import functools
 import math
 
 import jax
 import jax.numpy as jnp
 from jax import lax
+from jax.experimental import pallas as pl
+from jax.experimental.pallas import tpu as pltpu
 from jax.sharding import PartitionSpec as P
 
 D = 768
@@ -23,6 +26,558 @@
 RATE_VECTOR = 0.3
 DECAY = 0.1
 ADAM_EPSILON = 1e-08
+
+
+MESH = pl.DeviceIdType.MESH
+NZ, NY, NX = 4, 2, 2
+CHIPS = NZ * NY * NX
+SMALL = 256
+PIECES = (
+    (4, 48, 0, 48, 0, 128, "zxy"),
+    (0, 48, 0, 48, 0, 1152, "xzy"),
+    (1, 48, 0, 48, 0, 384, "yzx"),
+    (2, 48, 0, 48, 0, 768, "yzx"),
+    (2, 48, 0, 48, 768, 768, "zxy"),
+    (3, 192, 0, 48, 0, 384, "zxy"),
+    (3, 192, 48, 144, 0, 384, "zyx"),
+)
+WIDTHS = (2304, 768, 3072, 768, SMALL)
+OWN_ROWS = (24, 24, 24, 96, 24)
+AXIS = {"z": 0, "y": 1, "x": 2}
+
+
+def place():
+    dp, fs = lax.axis_index("dp"), lax.axis_index("fsdp")
+    return lax.div(dp, NY), lax.rem(dp, NY), lax.div(fs, 2), lax.rem(fs, 2)
+
+
+def device(z, y, x, core):
+    return (z * NY + y, x * 2 + core)
+
+
+def offsets():
+    found = [
+        (dz, dy, dx)
+        for dz in range(1 - NZ, NZ)
+        for dy in range(NY)
+        for dx in range(NX)
+    ]
+    return sorted(found, key=lambda d: (abs(d[0]) + d[1] + d[2], abs(d[0])))
+
+
+def last_axis(order, away):
+    last = -1
+    for number, axis in enumerate(order):
+        if away[AXIS[axis]] != 0:
+            last = number
+    return last
+
+
+def children(order, away):
+    last = last_axis(order, away)
+    found = []
+    for number, axis in enumerate(order):
+        if number < last:
+            continue
+        if axis == "z":
+            if number > last:
+                found += ["up", "down"]
+            else:
+                found += ["up"] if away[0] < 0 else ["down"]
+        elif number > last:
+            found.append(axis)
+    return found
+
+
+def exists(side, z):
+    return {"up": z < NZ - 1, "down": z > 0}.get(side)
+
+
+def neighbour(side, spot):
+    z, y, x, core = spot
+    return {
+        "up": device(z + 1, y, x, core),
+        "down": device(z - 1, y, x, core),
+        "y": device(z, 1 - y, x, core),
+        "x": device(z, y, 1 - x, core),
+        "core": device(z, y, x, 1 - core),
+    }[side]
+
+
+def guarded(condition, action):
+    if condition is None:
+        action()
+    else:
+        pl.when(condition)(action)
+
+
+def both(first, second):
+    if first is None:
+        return second
+    if second is None:
+        return first
+    return first & second
+
+
+def greet(spot):
+    barrier = pltpu.get_barrier_semaphore()
+    z = spot[0]
+    for side in ("up", "down", "x", "y", "core"):
+
+        def hello(side=side):
+            pl.semaphore_signal(
+                barrier, inc=1, device_id=neighbour(side, spot), device_id_type=MESH
+            )
+
+        guarded(exists(side, z), hello)
+    count = 3 + jnp.where(z < NZ - 1, 1, 0) + jnp.where(z > 0, 1, 0)
+    pl.semaphore_wait(barrier, count)
+
+
+def source_of(spot, away):
+    z, y, x, _ = spot
+    sz = z + away[0]
+    sy = 1 - y if away[1] else y
+    sx = 1 - x if away[2] else x
+    valid = None
+    if away[0] > 0:
+        valid = sz < NZ
+    elif away[0] < 0:
+        valid = sz >= 0
+    return sz, sy, sx, valid
+
+
+def chip_number(sz, sy, sx):
+    return (sz * NY + sy) * NX + sx
+
+
+def aligned(value, by):
+    return value if isinstance(value, int) else pl.multiple_of(value, by)
+
+
+def piece_view(ref, piece, chip, core):
+    number, chip_rows, low, rows, column, columns, order = piece
+    half = WIDTHS[number] // 2
+    return ref.at[
+        pl.ds(aligned(chip * chip_rows + low, 16), rows),
+        pl.ds(aligned(core * half + column, 128), columns),
+    ]
+
+
+def gather_kernel(layer, *refs):
+    masters = refs[:5]
+    wholes = refs[5:10]
+    mine = refs[10:15]
+    theirs = refs[15:20]
+    blocks = refs[20:25]
+    local_sem, pair_send, pair_recv, store_sem, send_sem, recv_sem, core_send, core_recv = refs[25:]
+    spot = place()
+    z, y, x, core = spot
+    me = chip_number(z, y, x)
+    partner = neighbour("core", spot)
+    loads = []
+    for number in range(5):
+        half = WIDTHS[number] // 2
+        loads.append(
+            pltpu.make_async_copy(
+                masters[number].at[layer, :, pl.ds(aligned(core * half, 128), half)],
+                mine[number],
+                local_sem.at[number],
+            )
+        )
+        loads[-1].start()
+    greet(spot)
+    swaps = []
+    for number in (4, 0, 1, 2, 3):
+        half = WIDTHS[number] // 2
+        swap = pltpu.make_async_remote_copy(
+            src_ref=masters[number].at[layer, :, pl.ds(aligned((1 - core) * half, 128), half)],
+            dst_ref=theirs[number],
+            send_sem=pair_send.at[number],
+            recv_sem=pair_recv.at[number],
+            device_id=partner,
+            device_id_type=MESH,
+        )
+        swap.start()
+        swaps.append((number, swap))
+
+    def relay(index, away, source, view):
+        piece = PIECES[index]
+        for side in children(piece[6], away):
+
+            def send(side=side):
+                pltpu.make_async_remote_copy(
+                    src_ref=view,
+                    dst_ref=piece_view(wholes[piece[0]], piece, source, core),
+                    send_sem=send_sem.at[index, ("up", "down", "x", "y").index(side)],
+                    recv_sem=recv_sem.at[index, source],
+                    device_id=neighbour(side, spot),
+                    device_id_type=MESH,
+                ).start()
+
+            guarded(exists(side, z), send)
+        pltpu.make_async_remote_copy(
+            src_ref=view,
+            dst_ref=piece_view(wholes[piece[0]], piece, source, core),
+            send_sem=core_send.at[index],
+            recv_sem=core_recv.at[index],
+            device_id=partner,
+            device_id_type=MESH,
+        ).start()
+
+    stores = []
+    for number, swap in swaps:
+        loads[number].wait()
+        swap.wait_recv()
+        rows = OWN_ROWS[number]
+        own, other = mine[number][...], theirs[number][...]
+        is_first = core == 0
+        block = jnp.concatenate(
+            [jnp.where(is_first, own, other), jnp.where(is_first, other, own)], axis=0
+        )
+        blocks[number][...] = block.astype(jnp.bfloat16)
+        for index, piece in enumerate(PIECES):
+            if piece[0] != number:
+                continue
+            view = blocks[number].at[pl.ds(piece[2], piece[3]), pl.ds(piece[4], piece[5])]
+            store = pltpu.make_async_copy(
+                view, piece_view(wholes[number], piece, me, core), store_sem.at[index]
+            )
+            store.start()
+            stores.append(store)
+            relay(index, (0, 0, 0), me, view)
+    for away in offsets():
+        if away == (0, 0, 0):
+            continue
+        for index, piece in enumerate(PIECES):
+            sz, sy, sx, valid = source_of(spot, away)
+            source = chip_number(sz, sy, sx)
+
+            def arrival(index=index, piece=piece, source=source):
+                view = piece_view(wholes[piece[0]], piece, source, core)
+                pltpu.make_async_remote_copy(
+                    src_ref=view,
+                    dst_ref=view,
+                    send_sem=send_sem.at[index, 0],
+                    recv_sem=recv_sem.at[index, source],
+                    device_id=partner,
+                    device_id_type=MESH,
+                ).wait_recv()
+                relay(index, away, source, view)
+
+            guarded(valid, arrival)
+    for store in stores:
+        store.wait()
+    for _, swap in swaps:
+        swap.wait_send()
+    for index, piece in enumerate(PIECES):
+        number, rows, columns = piece[0], piece[3], piece[5]
+
+        def span(chunks, core_at):
+            half = WIDTHS[number] // 2
+            return wholes[number].at[
+                pl.ds(0, chunks * rows), pl.ds(aligned(core_at * half + piece[4], 128), columns)
+            ]
+
+        def wait_send(chunks, sem):
+            pltpu.make_async_remote_copy(
+                src_ref=span(chunks, core),
+                dst_ref=span(chunks, core),
+                send_sem=sem,
+                recv_sem=recv_sem.at[index, 0],
+                device_id=partner,
+                device_id_type=MESH,
+            ).wait_send()
+
+        order = piece[6]
+        before = 1
+        for axis in order:
+            if axis == "z":
+                for at in range(NZ):
+
+                    @pl.when(z == at)
+                    def _(at=at):
+                        if at < NZ - 1:
+                            wait_send(before * (at + 1), send_sem.at[index, 0])
+                        if at > 0:
+                            wait_send(before * (NZ - at), send_sem.at[index, 1])
+
+                before *= NZ
+            else:
+                wait_send(before, send_sem.at[index, 2 if axis == "x" else 3])
+                before *= 2
+        wait_send(CHIPS, core_send.at[index])
+        pltpu.make_async_remote_copy(
+            src_ref=span(CHIPS, 1 - core),
+            dst_ref=span(CHIPS, 1 - core),
+            send_sem=core_send.at[index],
+            recv_sem=core_recv.at[index],
+            device_id=partner,
+            device_id_type=MESH,
+        ).wait_recv()
+
+
+def gather_layer(layer, masters, ident):
+    count = len(PIECES)
+    return pl.pallas_call(
+        functools.partial(gather_kernel, layer),
+        out_shape=tuple(
+            jax.ShapeDtypeStruct((32 * OWN_ROWS[n], WIDTHS[n]), jnp.bfloat16) for n in range(5)
+        ),
+        in_specs=[pl.BlockSpec(memory_space=pl.ANY)] * 5,
+        out_specs=tuple([pl.BlockSpec(memory_space=pl.ANY)] * 5),
+        scratch_shapes=(
+            [pltpu.VMEM((OWN_ROWS[n], WIDTHS[n] // 2), jnp.float32) for n in range(5)]
+            + [pltpu.VMEM((OWN_ROWS[n], WIDTHS[n] // 2), jnp.float32) for n in range(5)]
+            + [pltpu.VMEM((2 * OWN_ROWS[n], WIDTHS[n] // 2), jnp.bfloat16) for n in range(5)]
+            + [
+                pltpu.SemaphoreType.DMA((5,)),
+                pltpu.SemaphoreType.DMA((5,)),
+                pltpu.SemaphoreType.DMA((5,)),
+                pltpu.SemaphoreType.DMA((count,)),
+                pltpu.SemaphoreType.DMA((count, 4)),
+                pltpu.SemaphoreType.DMA((count, CHIPS)),
+                pltpu.SemaphoreType.DMA((count,)),
+                pltpu.SemaphoreType.DMA((count,)),
+            ]
+        ),
+        name=f"gather_{layer}",
+        compiler_params=pltpu.CompilerParams(
+            collective_id=ident, has_side_effects=True, vmem_limit_bytes=40 << 20
+        ),
+    )(*masters)
+
+
+def slot_of(order, side, source):
+    sizes = {"z": NZ, "y": NY, "x": NX}
+    base = 0
+    ahead = 1
+    number = 0
+    for axis in order:
+        at = source[AXIS[axis]]
+        for here in ["up", "down"] if axis == "z" else [axis]:
+            if axis == "z":
+                if here == side:
+                    return base + number * NZ + at
+                base += ahead * NZ
+            else:
+                if here == side:
+                    return base + number
+                base += ahead
+        number = number * sizes[axis] + at
+        ahead *= sizes[axis]
+    return base
+
+
+def slot_count(order):
+    return slot_of(order, None, (0, 0, 0))
+
+
+def scatter_kernel(*refs):
+    partials = refs[:5]
+    outs = refs[5:10]
+    count = len(PIECES)
+    own = refs[10:15]
+    pair = refs[15:20]
+    total = refs[20:25]
+    handed = refs[25:30]
+    slots = refs[30 : 30 + count]
+    (
+        own_sem,
+        pair_send,
+        pair_recv,
+        send_sem,
+        recv_sem,
+        end_send,
+        end_recv,
+        out_sem,
+    ) = refs[30 + count :]
+    spot = place()
+    z, y, x, core = spot
+    me = chip_number(z, y, x)
+    partner = neighbour("core", spot)
+    loads = []
+    for index, piece in enumerate(PIECES):
+        pass
+    for number in (4, 0, 1, 2, 3):
+        half = WIDTHS[number] // 2
+        load = pltpu.make_async_copy(
+            partials[number].at[:, pl.ds(aligned(core * half, 128), half)],
+            own[number],
+            own_sem.at[number],
+        )
+        load.start()
+        loads.append(load)
+    greet(spot)
+    swaps = []
+    for number in (4, 0, 1, 2, 3):
+        half = WIDTHS[number] // 2
+        swap = pltpu.make_async_remote_copy(
+            src_ref=partials[number].at[:, pl.ds(aligned((1 - core) * half, 128), half)],
+            dst_ref=pair[number],
+            send_sem=pair_send.at[number],
+            recv_sem=pair_recv.at[number],
+            device_id=partner,
+            device_id_type=MESH,
+        )
+        swap.start()
+        swaps.append(swap)
+    ready = set()
+    sides = ("up", "down", "x", "y")
+    for away in reversed(offsets()):
+        for index, piece in enumerate(PIECES):
+            number, chip_rows, low, rows, column, columns, order = piece
+            if number not in ready:
+                ready.add(number)
+                at = (4, 0, 1, 2, 3).index(number)
+                loads[at].wait()
+                swaps[at].wait_recv()
+            sz, sy, sx, valid = source_of(spot, away)
+            source = chip_number(sz, sy, sx)
+            last = last_axis(order, away)
+
+            def event(
+                index=index, number=number, chip_rows=chip_rows, low=low, rows=rows,
+                column=column, columns=columns, order=order, source=source, last=last,
+                where=(sz, sy, sx),
+            ):
+                kids = children(order, away)
+                for side in kids:
+
+                    def arrived(side=side):
+                        slot = slot_of(order, side, where)
+                        pltpu.make_async_remote_copy(
+                            src_ref=slots[index].at[slot],
+                            dst_ref=slots[index].at[slot],
+                            send_sem=send_sem.at[index, 0],
+                            recv_sem=recv_sem.at[index, slot],
+                            device_id=partner,
+                            device_id_type=MESH,
+                        ).wait_recv()
+
+                    guarded(exists(side, z), arrived)
+                view = (pl.ds(aligned(source * chip_rows + low, 16), rows), pl.ds(column, columns))
+                value = own[number][view].astype(jnp.float32) + pair[number][view].astype(jnp.float32)
+                for side in kids:
+                    landed = slots[index][slot_of(order, side, where)].astype(jnp.float32)
+                    there = exists(side, z)
+                    value = value + (landed if there is None else jnp.where(there, landed, 0.0))
+                if last < 0:
+                    total[number][pl.ds(low, rows), pl.ds(column, columns)] = value
+                    return
+                pair[number][view] = value.astype(jnp.bfloat16)
+                axis = order[last]
+                if axis == "z":
+                    side = "up" if away[0] < 0 else "down"
+                    parent = neighbour("down" if away[0] < 0 else "up", spot)
+                else:
+                    side = axis
+                    parent = neighbour(axis, spot)
+                slot = slot_of(order, side, where)
+                pltpu.make_async_remote_copy(
+                    src_ref=pair[number].at[view],
+                    dst_ref=slots[index].at[slot],
+                    send_sem=send_sem.at[index, source],
+                    recv_sem=recv_sem.at[index, slot],
+                    device_id=parent,
+                    device_id_type=MESH,
+                ).start()
+
+            guarded(valid, event)
+    ends = []
+    for number in range(5):
+        rows = OWN_ROWS[number]
+        end = pltpu.make_async_remote_copy(
+            src_ref=total[number].at[pl.ds(aligned((1 - core) * rows, 8), rows)],
+            dst_ref=handed[number],
+            send_sem=end_send.at[number],
+            recv_sem=end_recv.at[number],
+            device_id=partner,
+            device_id_type=MESH,
+        )
+        end.start()
+        ends.append(end)
+    writes = []
+    for number in range(5):
+        rows = OWN_ROWS[number]
+        half = WIDTHS[number] // 2
+        write = pltpu.make_async_copy(
+            total[number].at[pl.ds(aligned(core * rows, 8), rows)],
+            outs[number].at[:, pl.ds(aligned(core * half, 128), half)],
+            out_sem.at[number],
+        )
+        write.start()
+        writes.append(write)
+    for number in range(5):
+        half = WIDTHS[number] // 2
+        ends[number].wait_recv()
+        write = pltpu.make_async_copy(
+            handed[number],
+            outs[number].at[:, pl.ds(aligned((1 - core) * half, 128), half)],
+            out_sem.at[5 + number],
+        )
+        write.start()
+        writes.append(write)
+    for write in writes:
+        write.wait()
+    for end in ends:
+        end.wait_send()
+    for swap in swaps:
+        swap.wait_send()
+    for index, piece in enumerate(PIECES):
+        number, chip_rows, low, rows, column, columns, order = piece
+        for away in offsets():
+            if away == (0, 0, 0):
+                continue
+            sz, sy, sx, valid = source_of(spot, away)
+            source = chip_number(sz, sy, sx)
+
+            def sent(index=index, source=source):
+                view = (pl.ds(aligned(source * chip_rows + low, 16), rows), pl.ds(column, columns))
+                pltpu.make_async_remote_copy(
+                    src_ref=pair[number].at[view],
+                    dst_ref=slots[index].at[0],
+                    send_sem=send_sem.at[index, source],
+                    recv_sem=recv_sem.at[index, 0],
+                    device_id=partner,
+                    device_id_type=MESH,
+                ).wait_send()
+
+            guarded(valid, sent)
+
+
+def scatter_layer(layer, partials, ident):
+    count = len(PIECES)
+    most = max(slot_count(p[6]) for p in PIECES)
+    return pl.pallas_call(
+        scatter_kernel,
+        out_shape=tuple(
+            jax.ShapeDtypeStruct((OWN_ROWS[n], WIDTHS[n]), jnp.float32) for n in range(5)
+        ),
+        in_specs=[pl.BlockSpec(memory_space=pl.ANY)] * 5,
+        out_specs=tuple([pl.BlockSpec(memory_space=pl.ANY)] * 5),
+        scratch_shapes=(
+            [pltpu.VMEM((32 * OWN_ROWS[n], WIDTHS[n] // 2), jnp.bfloat16) for n in range(5)]
+            + [pltpu.VMEM((32 * OWN_ROWS[n], WIDTHS[n] // 2), jnp.bfloat16) for n in range(5)]
+            + [pltpu.VMEM((2 * OWN_ROWS[n], WIDTHS[n] // 2), jnp.float32) for n in range(5)]
+            + [pltpu.VMEM((OWN_ROWS[n], WIDTHS[n] // 2), jnp.float32) for n in range(5)]
+            + [pltpu.VMEM((slot_count(p[6]), p[3], p[5]), jnp.bfloat16) for p in PIECES]
+            + [
+                pltpu.SemaphoreType.DMA((5,)),
+                pltpu.SemaphoreType.DMA((5,)),
+                pltpu.SemaphoreType.DMA((5,)),
+                pltpu.SemaphoreType.DMA((count, CHIPS)),
+                pltpu.SemaphoreType.DMA((count, most)),
+                pltpu.SemaphoreType.DMA((5,)),
+                pltpu.SemaphoreType.DMA((5,)),
+                pltpu.SemaphoreType.DMA((10,)),
+            ]
+        ),
+        name=f"scatter_{layer}",
+        compiler_params=pltpu.CompilerParams(
+            collective_id=ident, has_side_effects=True, vmem_limit_bytes=56 << 20
+        ),
+    )(*partials)
 
 
 def with_halo(cells, sides, width):
@@ -95,36 +650,70 @@
     )
 
 
-def fetch_layer(masters, layer_index):
-    first_matrix = masters[0][layer_index].astype(jnp.bfloat16)
-    second_matrix = masters[1][layer_index].astype(jnp.bfloat16)
-    third_matrix = masters[2][layer_index].astype(jnp.bfloat16)
-    fourth_matrix = masters[3][layer_index].astype(jnp.bfloat16)
-    bias_part = masters[4][layer_index].astype(jnp.bfloat16)
-    table_part = jnp.transpose(masters[5][layer_index].astype(jnp.bfloat16))
-    whole = (
-        lax.all_gather(first_matrix, ("dp", "fsdp"), axis=0, tiled=True),
-        lax.all_gather(second_matrix, ("dp", "fsdp"), axis=0, tiled=True),
-        lax.all_gather(third_matrix, ("dp", "fsdp"), axis=0, tiled=True),
-        lax.all_gather(fourth_matrix, ("dp", "fsdp"), axis=0, tiled=True),
-        lax.all_gather(bias_part, ("dp", "fsdp"), axis=1, tiled=True),
-        lax.all_gather(table_part, ("dp", "fsdp"), axis=0, tiled=True),
-    )
-    return (whole[0], whole[1], whole[2], whole[3], whole[4], jnp.transpose(whole[5]))
-
-
-def reduce_layer(gradients):
-    grad_first, grad_second, grad_third, grad_fourth, grad_bias, grad_table = gradients
-    table_turned = jnp.transpose(grad_table)
-    summed = (
-        lax.psum_scatter(grad_first, ("dp", "fsdp"), scatter_dimension=0, tiled=True),
-        lax.psum_scatter(grad_second, ("dp", "fsdp"), scatter_dimension=0, tiled=True),
-        lax.psum_scatter(grad_third, ("dp", "fsdp"), scatter_dimension=0, tiled=True),
-        lax.psum_scatter(grad_fourth, ("dp", "fsdp"), scatter_dimension=0, tiled=True),
-        lax.psum_scatter(grad_bias, ("dp", "fsdp"), scatter_dimension=1, tiled=True),
-        lax.psum_scatter(table_turned, ("dp", "fsdp"), scatter_dimension=0, tiled=True),
-    )
-    return (summed[0], summed[1], summed[2], summed[3], summed[4], jnp.transpose(summed[5]))
+def direct():
+    return lax.axis_size("dp") == NZ * NY and lax.axis_size("fsdp") == NX * 2
+
+
+def pack_small(bias, table):
+    flat = jnp.concatenate([bias.reshape(LAYERS, -1), table.reshape(LAYERS, -1)], axis=1)
+    flat = jnp.pad(flat, ((0, 0), (0, OWN_ROWS[4] * SMALL - flat.shape[1])))
+    return flat.reshape(LAYERS, OWN_ROWS[4], SMALL)
+
+
+def unpack_small(whole):
+    count = lax.axis_size("dp") * lax.axis_size("fsdp")
+    flat = whole.reshape(count, -1)
+    wide = 9 * D // count
+    bias = flat[:, :wide].reshape(count, 9, -1).transpose(1, 0, 2).reshape(9, D)
+    table = flat[:, wide : wide + LEADS * 4 * D // count].reshape(count, LEADS, -1)
+    return bias, table.transpose(1, 0, 2).reshape(LEADS, 4 * D)
+
+
+def fetch_layers(masters):
+    if direct():
+        packed = tuple(masters[:4]) + (pack_small(masters[4], masters[5]),)
+        layers = []
+        for layer in range(LAYERS):
+            whole = gather_layer(layer, packed, layer)
+            layers.append(tuple(whole[:4]) + unpack_small(whole[4]))
+        return layers
+    both_axes = ("dp", "fsdp")
+    layers = []
+    for layer in range(LAYERS):
+        low = [m[layer].astype(jnp.bfloat16) for m in masters]
+        layers.append(
+            tuple(lax.all_gather(low[n], both_axes, axis=0, tiled=True) for n in range(4))
+            + tuple(lax.all_gather(low[n], both_axes, axis=1, tiled=True) for n in (4, 5))
+        )
+    return layers
+
+
+def reduce_layer(layer, gradients):
+    both_axes = ("dp", "fsdp")
+    if direct():
+        count = lax.axis_size("dp") * lax.axis_size("fsdp")
+        bias, table = gradients[4], gradients[5]
+        flat = jnp.concatenate(
+            [
+                bias.reshape(9, count, -1).transpose(1, 0, 2).reshape(count, -1),
+                table.reshape(LEADS, count, -1).transpose(1, 0, 2).reshape(count, -1),
+            ],
+            axis=1,
+        )
+        used = flat.shape[1]
+        small = jnp.pad(flat, ((0, 0), (0, OWN_ROWS[4] * SMALL - used))).reshape(-1, SMALL)
+        partials = tuple(g.astype(jnp.bfloat16) for g in (*gradients[:4], small))
+        summed = scatter_layer(layer, partials, LAYERS + layer)
+        flat = summed[4].reshape(-1)
+        wide = 9 * D // count
+        return tuple(summed[:4]) + (
+            flat[:wide].reshape(9, -1),
+            flat[wide:used].reshape(LEADS, -1),
+        )
+    return tuple(
+        lax.psum_scatter(gradients[n], both_axes, scatter_dimension=0 if n < 4 else 1, tiled=True)
+        for n in range(6)
+    )
 
 
 def build_masks(segment_ids, padding_mask, offset, row_count):
@@ -412,21 +1001,20 @@
         lead_table,
     )
     stream = tokens.astype(jnp.float32)
-    gathered_layers = []
     saved_layers = []
+    gathered_layers = fetch_layers(masters)
     for layer_index in range(LAYERS):
-        gathered = fetch_layer(masters, layer_index)
+        gathered = gathered_layers[layer_index]
         stream, saved_values = forward_layer(stream, gathered, context)
-        gathered_layers.append(gathered)
         saved_layers.append(saved_values)
     grad_stream = cotangent.astype(jnp.float32)
     reduced_layers = [None] * LAYERS
     for layer_index in reversed(range(LAYERS)):
-        gathered = fetch_layer(masters, layer_index)
+        gathered = gathered_layers[layer_index]
         grad_stream, layer_grads = backward_layer(
             grad_stream, gathered, saved_layers[layer_index], context
         )
-        reduced_layers[layer_index] = reduce_layer(layer_grads)
+        reduced_layers[layer_index] = reduce_layer(layer_index, layer_grads)
     moments = (input_moment, output_moment, expand_moment, shrink_moment, bias_moment, lead_moment)
     squares = (input_square, output_square, expand_square, shrink_square, bias_square, lead_square)
     results = []

time: 2040 us -> 926 us (0.45)
  waiting for transfers between devices: 1170 us -> 0.34 us
  Pallas kernels: 0 us -> 295 us
  blocking collectives: 219 us -> 0 us
  matrix products: 350 us -> 320 us
    reduce_scatter x8 -> x0, waiting for transfers between devices: 1010 us -> none  [the longest x2 279 us: reduce_layer(): lax.psum_scatter(grad_fourth, ('dp', 'fsdp'), scatter_dimension=0, tiled=...]
    pallas_call x0 -> x4, Pallas kernels: none -> 295 us  [the longest x2 154 us: scatter_layer(): pl.pallas_call(scatter_kernel, out_shape=tuple((jax.ShapeDtypeStruct((OWN...]
    all_gather x4 -> x0, blocking collectives: 170 us -> none  [the longest x2 88.5 us: fetch_layer(): lax.all_gather(bias_part, ('dp', 'fsdp'), axis=1, tiled=True)]
    unnamed x20 -> x0, waiting for transfers between devices: 79.6 us -> none
    all_gather x8 -> x0, waiting for transfers between devices: 78.4 us -> none  [the longest x2 46.2 us: fetch_layer(): lax.all_gather(fourth_matrix, ('dp', 'fsdp'), axis=0, tiled=True)]
    unnamed x1 -> x0, blocking collectives: 49.4 us -> none
  transfers between devices with their start and end apart: 26 -> 8, of which waited for: 12 -> 1; matrix products, arithmetic and copies ran while one was open for 17% -> 4% of each run, Pallas kernels for 0% -> 8%
where the time goes in v1:
time: 926 us; the launch traced here: 908 us
  matrix products  320 us (35%)
  Pallas kernels  295 us (32%)
  other arithmetic  146 us (16%)
  local copies, waits for them, and re-layouts  98.1 us (11%)
  starting transfers between devices  45.2 us (5%)
    pallas_call x2, Pallas kernels, scatter_layer(): pl.pallas_call(scatter_kernel, out_shape=tuple((jax.ShapeDtypeStruct((OWN...  154 us
    pallas_call x2, Pallas kernels, gather_layer(): pl.pallas_call(functools.partial(gather_kernel, layer), out_shape=tuple((...  141 us
    dot_general x2, matrix products, attend_backward(): jnp.einsum('qhd,khd->hqk', grad_attended, value_block, preferred_element_...  57.8 us
    convert_element_type x2, other arithmetic, attend_backward(): (probabilities * (grad_weights - row_delta)).astype(jnp.bfloat16)  48.7 us
    dot_general x2, matrix products, forward_layer(): jnp.dot(input_two, expand_full, preferred_element_type=jnp.float32)  40 us
    dot_general x2, matrix products, attend_backward(): jnp.einsum('hqk,qhd->khd', weights, grad_attended, preferred_element_type...  36.4 us
    reduce_sum x2, other arithmetic, attend_forward(): jnp.sum(jnp.exp(masked - row_peak), axis=-1, keepdims=True)  34.8 us
    ppermute x4, starting transfers between devices, passed_along(): return lax.ppermute(value, axis, pairs)  34.2 us
  transfers between devices with their start and end apart: 8, of which 1 were waited for; matrix products, arithmetic and copies ran while one was open for 4% of the time, Pallas kernels for 8%

profile of v1, /device:TPU:0, one launch (start us, length us, event | category | flops | bytes accessed | tf_op | source)
XLA Modules:
  0.0 908.4 jit_solution(8611726845991583606)
XLA Ops:
  6.4 67.6 %gather_0.1 = (bf16[768,2304]{1,0:T(8,128)(2,1)S(1)}, bf16[768,768]{1,0:T(8,128)(2,1)S(1)}, bf16[768,3072]{1,0:T(8,128)(2,1)S(1)}, bf16[3072,768]{1,0:T(8,128)(2,1)}, bf16[768,256]{1,0:T(8,128)(2,1)S(1)}) custom-call(f32[2,24,2304]{2,1,0:T(8,128)S(1)} %copy-done.4, f32[2,24,768]{2,1,0:T(8,128)S(1)} %copy-done.6, f32[2,24,3072]{2,1,0:T(8,128)S(1)} %copy-done, ...), custom_call_target="tpu_custom_call" | custom-call | tf_op jit(solution)/shard_map/gather_0/pallas_call | solution.py:322
  112.8 73.7 %gather_1.1 = (bf16[768,2304]{1,0:T(8,128)(2,1)S(1)}, bf16[768,768]{1,0:T(8,128)(2,1)S(1)}, bf16[768,3072]{1,0:T(8,128)(2,1)S(1)}, bf16[3072,768]{1,0:T(8,128)(2,1)}, bf16[768,256]{1,0:T(8,128)(2,1)S(1)}) custom-call(f32[2,24,2304]{2,1,0:T(8,128)S(1)} %copy-done.5, f32[2,24,768]{2,1,0:T(8,128)S(1)} %copy-done.7, f32[2,24,3072]{2,1,0:T(8,128)S(1)} %copy-done.1, ...), custom_call_target="tpu_custom_call" | custom-call | tf_op jit(solution)/shard_map/gather_1/pallas_call | solution.py:322
  217.1 17.2 %fusion = (f32[12,512]{1,0:T(8,128)S(1)}, f32[12,512,1536]{2,1,0:T(8,128)}) fusion(pred[512,1536]{1,0:T(8,128)(4,1)} %fusion.31, bf16[1536,12,64]{0,2,1:T(8,128)(2,1)} %bitcast.148, bf16[512,12,32]{0,2,1:T(8,128)(2,1)} %get-tuple-element.295, bf16[512,12,32]{0,2,1:T(8,128)(2,1)S(1)} %copy-done.43), kind=kOutput, calls=%fused_computation.10 | convolution fusion | flops 1237837824 | bytes 41705472 | tf_op jit(solution)/shard_map/qhd,khd->hqk/dot_general | solution.py:739
  234.3 17.4 %exponential_reduce_fusion.1 = f32[12,512]{1,0:T(8,128)S(1)} fusion(f32[12,512,1536]{2,1,0:T(8,128)} %get-tuple-element.316, f32[12,512]{1,0:T(8,128)S(1)} %get-tuple-element.315, pred[512,1536]{1,0:T(8,128)(4,1)S(1)} %copy-done.21), kind=kLoop, calls=%fused_computation.8 | loop fusion | flops 37742592 | bytes 38584320 | tf_op jit(solution)/shard_map/reduce_sum | solution.py:760
  251.8 16.7 %convolution_convert_fusion.11 = bf16[12,64,512]{2,1,0:T(8,128)(2,1)S(1)} fusion(bf16[1536,12,64]{0,2,1:T(8,128)(2,1)S(1)} %bitcast.163, f32[12,512,1536]{2,1,0:T(8,128)} %get-tuple-element.316, f32[12,512]{1,0:T(8,128)S(1)} %log_add_fusion.1, pred[512,1536]{1,0:T(8,128)(4,1)S(1)} %copy-done.21), kind=kOutput, calls=%fused_computation.137 | convolution fusion | flops 1246101504 | bytes 41705472 | tf_op jit(solution)/shard_map/hqk,khd->qhd/dot_general | solution.py:763
  270.0 18.7 %multiply_convert_fusion.3 = (bf16[512,3072]{1,0:T(8,128)(2,1)S(1)}, f32[512,3072]{1,0:T(8,128)}, f32[512,3072]{1,0:T(8,128)}) fusion(f32[3072]{0:T(1024)S(1)} %add.439, bf16[768,3072]{1,0:T(8,128)(2,1)S(1)} %bitcast.143, f32[512,768]{1,0:T(8,128)S(1)} %get-tuple-element.318, f32[768]{0:T(1024)S(1)} %get-tuple-element.233, f32[768]{0:T(1024)S(1)} %get-tuple-element.232, ...), kind=kOutput, calls=%fused_computation.49 | convolution fusion | flops 2521694208 | bytes 22042624 | tf_op jit(solution)/shard_map/dot_general | solution.py:840
  330.9 17.0 %fusion.1 = (f32[12,512]{1,0:T(8,128)S(1)}, f32[12,512,1536]{2,1,0:T(8,128)}) fusion(pred[512,1536]{1,0:T(8,128)(4,1)S(1)} %copy-done.22, bf16[1536,12,64]{0,2,1:T(8,128)(2,1)} %bitcast.150, bf16[512,12,32]{0,2,1:T(8,128)(2,1)S(1)} %copy-done.47, bf16[512,12,32]{0,2,1:T(8,128)(2,1)S(1)} %copy-done.45), kind=kOutput, calls=%fused_computation.11 | convolution fusion | flops 1237837824 | bytes 41705472 | tf_op jit(solution)/shard_map/qhd,khd->hqk/dot_general | solution.py:739
  347.9 17.3 %exponential_reduce_fusion = f32[12,512]{1,0:T(8,128)S(1)} fusion(f32[12,512,1536]{2,1,0:T(8,128)} %get-tuple-element.323, f32[12,512]{1,0:T(8,128)S(1)} %get-tuple-element.322, pred[512,1536]{1,0:T(8,128)(4,1)S(1)} %copy-done.22), kind=kLoop, calls=%fused_computation.5 | loop fusion | flops 37742592 | bytes 38584320 | tf_op jit(solution)/shard_map/reduce_sum | solution.py:760
  365.3 16.6 %convolution_convert_fusion.10 = bf16[12,64,512]{2,1,0:T(8,128)(2,1)S(1)} fusion(bf16[1536,12,64]{0,2,1:T(8,128)(2,1)S(1)} %bitcast.165, f32[12,512,1536]{2,1,0:T(8,128)} %get-tuple-element.323, f32[12,512]{1,0:T(8,128)S(1)} %log_add_fusion, pred[512,1536]{1,0:T(8,128)(4,1)S(1)} %copy-done.22), kind=kOutput, calls=%fused_computation.136 | convolution fusion | flops 1246101504 | bytes 41705472 | tf_op jit(solution)/shard_map/hqk,khd->qhd/dot_general | solution.py:763
  383.3 21.2 %multiply_convert_fusion.2 = (bf16[512,3072]{1,0:T(8,128)(2,1)}, f32[512,3072]{1,0:T(8,128)}, f32[512,3072]{1,0:T(8,128)}) fusion(f32[3072]{0:T(1024)S(1)} %add.466, bf16[768,3072]{1,0:T(8,128)(2,1)S(1)} %bitcast.147, f32[512,768]{1,0:T(8,128)S(1)} %get-tuple-element.325, f32[768]{0:T(1024)S(1)} %copy-done.126, f32[768]{0:T(1024)S(1)} %copy-done.104, ...), kind=kOutput, calls=%fused_computation.36 | convolution fusion | flops 2521694208 | bytes 22042624 | tf_op jit(solution)/shard_map/dot_general | solution.py:840
  404.6 8.2 fusion.129
  421.5 28.5 %multiply_reduce_fusion.1 = (f32[12,512]{1,0:T(8,128)S(1)}, f32[12,512,1536]{2,1,0:T(8,128)}) fusion(f32[12,512,1536]{2,1,0:T(8,128)} %get-tuple-element.323, f32[12,512]{1,0:T(8,128)S(1)} %log_add_fusion, pred[512,1536]{1,0:T(8,128)(4,1)S(1)} %copy-done.22, bf16[512,12,64]{0,2,1:T(8,128)(2,1)S(1)} %bitcast.172, bf16[1536,12,64]{0,2,1:T(8,128)(2,1)} %bitcast.164), kind=kOutput, calls=%fused_computation.3 | convolution fusion | flops 1255139328 | bytes 79478784 | tf_op jit(solution)/shard_map/qhd,khd->hqk/dot_general | solution.py:785
  450.0 18.4 %fusion.58 = f32[12,64,1536]{2,1,0:T(8,128)} fusion(bf16[512,12,64]{0,2,1:T(8,128)(2,1)S(1)} %bitcast.173, f32[12,512,1536]{2,1,0:T(8,128)} %get-tuple-element.323, f32[12,512]{1,0:T(8,128)S(1)} %log_add_fusion, pred[512,1536]{1,0:T(8,128)(4,1)S(1)} %copy-done.22), kind=kOutput, calls=%fused_computation.201 | convolution fusion | flops 1245708288 | bytes 44064768 | tf_op jit(solution)/shard_map/hqk,qhd->khd/dot_general | solution.py:797
  487.5 24.5 %multiply_convert_fusion.1 = bf16[12,512,1536]{2,1,0:T(8,128)(2,1)S(1)} fusion(f32[12,512,1536]{2,1,0:T(8,128)} %get-tuple-element.329, f32[12,512,1536]{2,1,0:T(8,128)} %get-tuple-element.323, f32[12,512]{1,0:T(8,128)S(1)} %get-tuple-element.328, f32[12,512]{1,0:T(8,128)S(1)} %log_add_fusion, pred[512,1536]{1,0:T(8,128)(4,1)S(1)} %copy-done.22), kind=kLoop, calls=%fused_computation.2 | loop fusion | flops 56623104 | bytes 95207424 | tf_op jit(solution)/shard_map/convert_element_type | solution.py:789
  527.3 19.6 %collective-permute-start.4 = (bf16[512,1536]{0,1:T(8,128)(2,1)}, bf16[512,1536]{0,1:T(8,128)(2,1)}, u32[]{:S(2)}, u32[]{:S(2)}) collective-permute-start(bf16[512,1536]{0,1:T(8,128)(2,1)} %get-tuple-element.272), channel_id=1, source_target_pairs={{0,1},{1,2},{2,3},{4,5},{5,6},{6,7},{8,9},{9,10},{10,11},{12,13},{... | collective-permute-start | bytes 4718600 | tf_op jit(solution)/shard_map/ppermute | solution.py:603
  547.0 10.5 %multiply_bitcast_fusion.1 = f32[512,12,64]{0,2,1:T(8,128)S(1)} fusion(bf16[1536,12,64]{0,2,1:T(8,128)(2,1)} %bitcast.151, bf16[12,512,1536]{2,1,0:T(8,128)(2,1)} %copy-done.20), kind=kOutput, calls=%fused_computation.117 | convolution fusion | flops 1208352768 | bytes 22806528 | tf_op jit(solution)/shard_map/hqk,khd->qhd/dot_general | solution.py:791
  569.0 9.8 %fusion.130 = (bf16[3072]{0:T(1024)(128)(2,1)}, bf16[512,3072]{1,0:T(8,128)(2,1)S(1)}) fusion(f32[512,3072]{1,0:T(8,128)} %get-tuple-element.269, bf16[3072,768]{1,0:T(8,128)(2,1)} %get-tuple-element.170, f32[512,768]{1,0:T(8,128)S(1)} %get-tuple-element.263, f32[512,3072]{1,0:T(8,128)} %get-tuple-element.319, f32[3072]{0:T(1024)S(1)} %copy-done.106), kind=kOutput, calls=%fused_computation.318 | convolution fusion | flops 2441475072 | bytes 22038528 | tf_op jit(solution)/shard_map/td,fd->tf/dot_general | solution.py:889
  587.3 29.4 %multiply_reduce_fusion = (f32[12,512]{1,0:T(8,128)}, f32[12,512,1536]{2,1,0:T(8,128)}) fusion(f32[12,512,1536]{2,1,0:T(8,128)} %get-tuple-element.316, f32[12,512]{1,0:T(8,128)S(1)} %copy-done.71, pred[512,1536]{1,0:T(8,128)(4,1)S(1)} %copy-done.22, bf16[512,12,64]{0,2,1:T(8,128)(2,1)S(1)} %bitcast.174, bf16[1536,12,64]{0,2,1:T(8,128)(2,1)} %bitcast.162), kind=kOutput, calls=%fused_computation.1 | convolution fusion | flops 1255139328 | bytes 79478784 | tf_op jit(solution)/shard_map/qhd,khd->hqk/dot_general | solution.py:785
  616.6 18.1 %fusion.61 = f32[12,64,1536]{2,1,0:T(8,128)} fusion(bf16[512,12,64]{0,2,1:T(8,128)(2,1)S(1)} %bitcast.175, f32[12,512,1536]{2,1,0:T(8,128)} %get-tuple-element.316, f32[12,512]{1,0:T(8,128)S(1)} %copy-done.71, pred[512,1536]{1,0:T(8,128)(4,1)S(1)} %copy-done.22), kind=kOutput, calls=%fused_computation.202 | convolution fusion | flops 1245708288 | bytes 44064768 | tf_op jit(solution)/shard_map/hqk,qhd->khd/dot_general | solution.py:797
  652.2 24.3 %multiply_convert_fusion = bf16[12,512,1536]{2,1,0:T(8,128)(2,1)S(1)} fusion(f32[12,512,1536]{2,1,0:T(8,128)} %get-tuple-element.333, f32[12,512,1536]{2,1,0:T(8,128)} %get-tuple-element.316, f32[12,512]{1,0:T(8,128)S(1)} %copy-done.86, f32[12,512]{1,0:T(8,128)S(1)} %copy-done.72, pred[512,1536]{1,0:T(8,128)(4,1)S(1)} %copy-done.22), kind=kLoop, calls=%fused_computation | loop fusion | flops 56623104 | bytes 95207424 | tf_op jit(solution)/shard_map/convert_element_type | solution.py:789
  694.9 12.1 %collective-permute-start.6 = (bf16[512,1536]{0,1:T(8,128)(2,1)}, bf16[512,1536]{0,1:T(8,128)(2,1)}, u32[]{:S(2)}, u32[]{:S(2)}) collective-permute-start(bf16[512,1536]{0,1:T(8,128)(2,1)} %get-tuple-element.270), channel_id=1, source_target_pairs={{0,1},{1,2},{2,3},{4,5},{5,6},{6,7},{8,9},{9,10},{10,11},{12,13},{... | collective-permute-start | bytes 4718600 | tf_op jit(solution)/shard_map/ppermute | solution.py:603
  707.4 10.6 %multiply_bitcast_fusion = f32[512,12,64]{0,2,1:T(8,128)S(1)} fusion(bf16[1536,12,64]{0,2,1:T(8,128)(2,1)} %bitcast.149, bf16[12,512,1536]{2,1,0:T(8,128)(2,1)} %copy-done.19), kind=kOutput, calls=%fused_computation.112 | convolution fusion | flops 1208352768 | bytes 22806528 | tf_op jit(solution)/shard_map/hqk,khd->qhd/dot_general | solution.py:791
  735.3 83.3 %scatter_0.1 = (f32[24,2304]{1,0:T(8,128)}, f32[24,768]{1,0:T(8,128)}, f32[24,3072]{1,0:T(8,128)}, f32[96,768]{1,0:T(8,128)}, f32[24,256]{1,0:T(8,128)}) custom-call(bf16[768,2304]{1,0:T(8,128)(2,1)} %convolution_convert_fusion.5.refs_0_, bf16[768,768]{1,0:T(8,128)(2,1)} %convolution_convert_fusion.7.refs_1_, ...), custom_call_target="tpu_custom_call" | custom-call | tf_op jit(solution)/shard_map/scatter_0/pallas_call | solution.py:552
  820.9 70.2 %scatter_1.1 = (f32[24,2304]{1,0:T(8,128)}, f32[24,768]{1,0:T(8,128)}, f32[24,3072]{1,0:T(8,128)}, f32[96,768]{1,0:T(8,128)}, f32[24,256]{1,0:T(8,128)}) custom-call(bf16[768,2304]{1,0:T(8,128)(2,1)} %convolution_convert_fusion.2.refs_0_, bf16[768,768]{1,0:T(8,128)(2,1)} %convolution_convert_fusion.6.refs_1_, ...), custom_call_target="tpu_custom_call" | custom-call | tf_op jit(solution)/shard_map/scatter_1/pallas_call | solution.py:552
  (535 shorter events, 253.7 us)
Async XLA Ops:
  78.0 190.5 %copy-start.15 = (bf16[768,768]{1,0:T(8,128)(2,1)}, bf16[768,768]{1,0:T(8,128)(2,1)S(1)}, u32[]{:S(2)}) copy-start(bf16[768,768]{1,0:T(8,128)(2,1)S(1)} %get-tuple-element.168) | copy-start | bytes 3538948
  80.4 189.5 %copy-start.100 = (f32[768]{0:T(1024)}, f32[768]{0:T(1024)S(1)}, u32[]{:S(2)}) copy-start(f32[768]{0:T(1024)S(1)} %get-tuple-element.232) | copy-start | bytes 9220
  80.5 189.4 %copy-start.122 = (f32[768]{0:T(1024)}, f32[768]{0:T(1024)S(1)}, u32[]{:S(2)}) copy-start(f32[768]{0:T(1024)S(1)} %get-tuple-element.233) | copy-start | bytes 9220
  95.8 206.3 %copy-start.55 = (f32[512,32]{0,1:T(8,128)}, f32[512,32]{0,1:T(8,128)S(1)}, u32[]{:S(2)}) copy-start(f32[512,32]{0,1:T(8,128)S(1)} %get-tuple-element.313) | copy-start | bytes 196612
  95.8 206.3 %copy-start.58 = (f32[512,32]{0,1:T(8,128)}, f32[512,32]{0,1:T(8,128)S(1)}, u32[]{:S(2)}) copy-start(f32[512,32]{0,1:T(8,128)S(1)} %get-tuple-element.314) | copy-start | bytes 196612
  105.1 97.6 %collective-permute-start.1 = (bf16[512,1536]{1,0:T(8,128)(2,1)}, bf16[512,1536]{1,0:T(8,128)(2,1)}, u32[]{:S(2)}, u32[]{:S(2)}) collective-permute-start(bf16[512,1536]{1,0:T(8,128)(2,1)} %pad_maximum_fusion.6), channel_id=1, source_target_pairs={{1,0},{2,1},{3,2},{5,4},{6,5},{7,6},{9,8},{10,9},{11,10},{13,12},{... | collective-permute-start | bytes 4718600 | tf_op jit(solution)/shard_map/ppermute | solution.py:593
  106.4 96.3 %collective-permute-start = (bf16[512,1536]{1,0:T(8,128)(2,1)}, bf16[512,1536]{1,0:T(8,128)(2,1)}, u32[]{:S(2)}, u32[]{:S(2)}) collective-permute-start(bf16[512,1536]{1,0:T(8,128)(2,1)} %pad_maximum_fusion.6), channel_id=1, source_target_pairs={{0,1},{1,2},{2,3},{4,5},{5,6},{6,7},{8,9},{9,10},{10,11},{12,13},{... | collective-permute-start | bytes 4718600 | tf_op jit(solution)/shard_map/ppermute | solution.py:591
  197.5 72.4 %copy-start.105 = (f32[3072]{0:T(1024)}, f32[3072]{0:T(1024)S(1)}, u32[]{:S(2)}) copy-start(f32[3072]{0:T(1024)S(1)} %add.439) | copy-start | bytes 36868
  200.8 91.0 %copy-start.102 = (f32[768]{0:T(1024)}, f32[768]{0:T(1024)S(1)}, u32[]{:S(2)}) copy-start(f32[768]{0:T(1024)S(1)} %get-tuple-element.231) | copy-start | bytes 9220
  309.0 7.4 collective-permute-start.3
  310.3 6.4 collective-permute-start.2
  382.9 33.0 %copy-start.39 = (f32[512,768]{1,0:T(8,128)}, f32[512,768]{1,0:T(8,128)S(1)}, u32[]{:S(2)}) copy-start(f32[512,768]{1,0:T(8,128)S(1)} %get-tuple-element.325) | copy-start | bytes 4718596
  526.0 31.5 %collective-permute-start.5 = (bf16[512,1536]{0,1:T(8,128)(2,1)}, bf16[512,1536]{0,1:T(8,128)(2,1)}, u32[]{:S(2)}, u32[]{:S(2)}) collective-permute-start(bf16[512,1536]{0,1:T(8,128)(2,1)} %get-tuple-element.273), channel_id=1, source_target_pairs={{1,0},{2,1},{3,2},{5,4},{6,5},{7,6},{9,8},{10,9},{11,10},{13,12},{... | collective-permute-start | bytes 4718600 | tf_op jit(solution)/shard_map/ppermute | solution.py:603
  527.3 30.2 %collective-permute-start.4 = (bf16[512,1536]{0,1:T(8,128)(2,1)}, bf16[512,1536]{0,1:T(8,128)(2,1)}, u32[]{:S(2)}, u32[]{:S(2)}) collective-permute-start(bf16[512,1536]{0,1:T(8,128)(2,1)} %get-tuple-element.272), channel_id=1, source_target_pairs={{0,1},{1,2},{2,3},{4,5},{5,6},{6,7},{8,9},{9,10},{10,11},{12,13},{... | collective-permute-start | bytes 4718600 | tf_op jit(solution)/shard_map/ppermute | solution.py:603
  693.6 24.5 %collective-permute-start.7 = (bf16[512,1536]{0,1:T(8,128)(2,1)}, bf16[512,1536]{0,1:T(8,128)(2,1)}, u32[]{:S(2)}, u32[]{:S(2)}) collective-permute-start(bf16[512,1536]{0,1:T(8,128)(2,1)} %get-tuple-element.271), channel_id=1, source_target_pairs={{1,0},{2,1},{3,2},{5,4},{6,5},{7,6},{9,8},{10,9},{11,10},{13,12},{... | collective-permute-start | bytes 4718600 | tf_op jit(solution)/shard_map/ppermute | solution.py:603
  694.9 23.2 %collective-permute-start.6 = (bf16[512,1536]{0,1:T(8,128)(2,1)}, bf16[512,1536]{0,1:T(8,128)(2,1)}, u32[]{:S(2)}, u32[]{:S(2)}) collective-permute-start(bf16[512,1536]{0,1:T(8,128)(2,1)} %get-tuple-element.270), channel_id=1, source_target_pairs={{0,1},{1,2},{2,3},{4,5},{5,6},{6,7},{8,9},{9,10},{10,11},{12,13},{... | collective-permute-start | bytes 4718600 | tf_op jit(solution)/shard_map/ppermute | solution.py:603
  735.3 84.2 %copy-start.116 = (bf16[768]{0:T(1024)(128)(2,1)S(1)}, bf16[768]{0:T(1024)(128)(2,1)}, u32[]{:S(2)}) copy-start(bf16[768]{0:T(1024)(128)(2,1)} %get-tuple-element.264) | copy-start | bytes 4612
  735.3 84.2 %copy-start.117 = (bf16[768]{0:T(1024)(128)(2,1)S(1)}, bf16[768]{0:T(1024)(128)(2,1)}, u32[]{:S(2)}) copy-start(bf16[768]{0:T(1024)(128)(2,1)} %get-tuple-element.298) | copy-start | bytes 4612
  735.3 84.2 %copy-start.118 = (bf16[3072]{0:T(1024)(128)(2,1)S(1)}, bf16[3072]{0:T(1024)(128)(2,1)}, u32[]{:S(2)}) copy-start(bf16[3072]{0:T(1024)(128)(2,1)} %get-tuple-element.335) | copy-start | bytes 18436
  820.9 71.2 %copy-start.90 = (f32[2,9,24]{2,0,1:T(2,128)S(1)}, f32[2,9,24]{2,0,1:T(2,128)}, u32[]{:S(2)}) copy-start(f32[2,9,24]{2,0,1:T(2,128)} %param.66) | copy-start | bytes 5188
  820.9 71.3 %copy-start.107 = (f32[2,9,24]{2,0,1:T(2,128)S(1)}, f32[2,9,24]{2,0,1:T(2,128)}, u32[]{:S(2)}) copy-start(f32[2,9,24]{2,0,1:T(2,128)} %param.67) | copy-start | bytes 5188
  820.9 71.3 %copy-start.108 = (f32[2,9,24]{2,0,1:T(2,128)S(1)}, f32[2,9,24]{2,0,1:T(2,128)}, u32[]{:S(2)}) copy-start(f32[2,9,24]{2,0,1:T(2,128)} %param.68) | copy-start | bytes 5188
  820.9 73.9 %copy-start.87 = (f32[2,20,96]{2,0,1:T(2,128)S(1)}, f32[2,20,96]{2,0,1:T(2,128)}, u32[]{:S(2)}) copy-start(f32[2,20,96]{2,0,1:T(2,128)} %param.69) | copy-start | bytes 46084
  820.9 78.0 %copy-start.26 = (f32[512,768]{1,0:T(8,128)S(1)}, f32[512,768]{1,0:T(8,128)}, u32[]{:S(2)}) copy-start(f32[512,768]{1,0:T(8,128)} %copy-done.24) | copy-start | bytes 4718596
  (138 other events, 1161.5 us)

commit v2 on v1

v2 whole, which is shorter than its diff:
```python
import functools
import math

import jax
import jax.numpy as jnp
from jax import lax
from jax.experimental import pallas as pl
from jax.experimental.pallas import tpu as pltpu
from jax.sharding import PartitionSpec as P

D = 768
FF = 3072
HEADS = 12
HEAD_DIM = 64
LEADS = 20
LAYERS = 2
WIN_MAX = 512
STEP = 10
LATER_OFFLOADED = True

EPSILON = 1e-06
NEGATIVE = -1e30
BETA_ONE = 0.5
BETA_TWO = 0.5
RATE_MATRIX = 0.08
RATE_VECTOR = 0.3
DECAY = 0.1
ADAM_EPSILON = 1e-08

MESH = pl.DeviceIdType.MESH
NZ, NY, NX = 4, 2, 2
CHIPS = NZ * NY * NX
SMALL = 256
PIECES = (
    (4, 2, 0, 48, 0, 48, 0, 128, "zxy"),
    (0, 0, 0, 48, 0, 48, 0, 1152, "xzy"),
    (1, 0, 2304, 48, 0, 48, 0, 384, "yzx"),
    (2, 0, 3072, 48, 0, 48, 0, 768, "yzx"),
    (2, 0, 3072, 48, 0, 48, 768, 768, "zxy"),
    (3, 1, 0, 192, 0, 48, 0, 384, "zxy"),
    (3, 1, 0, 192, 48, 144, 0, 384, "zyx"),
)
WIDTHS = (2304, 768, 3072, 768, SMALL)
OWN_ROWS = (24, 24, 24, 96, 24)
WHOLES = ((768, 6144), (3072, 768), (768, SMALL))
AXIS = {"z": 0, "y": 1, "x": 2}


def place():
    dp, fs = lax.axis_index("dp"), lax.axis_index("fsdp")
    return lax.div(dp, NY), lax.rem(dp, NY), lax.div(fs, 2), lax.rem(fs, 2)


def device(z, y, x, core):
    return (z * NY + y, x * 2 + core)


def offsets():
    found = [
        (dz, dy, dx)
        for dz in range(1 - NZ, NZ)
        for dy in range(NY)
        for dx in range(NX)
    ]
    return sorted(found, key=lambda d: (abs(d[0]) + d[1] + d[2], abs(d[0])))


def last_axis(order, away):
    last = -1
    for number, axis in enumerate(order):
        if away[AXIS[axis]] != 0:
            last = number
    return last


def children(order, away):
    last = last_axis(order, away)
    found = []
    for number, axis in enumerate(order):
        if number < last:
            continue
        if axis == "z":
            if number > last:
                found += ["up", "down"]
            else:
                found += ["up"] if away[0] < 0 else ["down"]
        elif number > last:
            found.append(axis)
    return found


def exists(side, z):
    return {"up": z < NZ - 1, "down": z > 0}.get(side)


def neighbour(side, spot):
    z, y, x, core = spot
    return {
        "up": device(z + 1, y, x, core),
        "down": device(z - 1, y, x, core),
        "y": device(z, 1 - y, x, core),
        "x": device(z, y, 1 - x, core),
        "core": device(z, y, x, 1 - core),
    }[side]


def guarded(condition, action):
    if condition is None:
        action()
    else:
        pl.when(condition)(action)


def both(first, second):
    if first is None:
        return second
    if second is None:
        return first
    return first & second


def greet(spot):
    barrier = pltpu.get_barrier_semaphore()
    z = spot[0]
    for side in ("up", "down", "x", "y", "core"):

        def hello(side=side):
            pl.semaphore_signal(
                barrier, inc=1, device_id=neighbour(side, spot), device_id_type=MESH
            )

        guarded(exists(side, z), hello)
    count = 3 + jnp.where(z < NZ - 1, 1, 0) + jnp.where(z > 0, 1, 0)
    pl.semaphore_wait(barrier, count)


def source_of(spot, away):
    z, y, x, _ = spot
    sz = z + away[0]
    sy = 1 - y if away[1] else y
    sx = 1 - x if away[2] else x
    valid = None
    if away[0] > 0:
        valid = sz < NZ
    elif away[0] < 0:
        valid = sz >= 0
    return sz, sy, sx, valid


def chip_number(sz, sy, sx):
    return (sz * NY + sy) * NX + sx


def aligned(value, by):
    return value if isinstance(value, int) else pl.multiple_of(value, by)


def piece_view(ref, piece, chip, core):
    number, _, base, chip_rows, low, rows, column, columns, _ = piece
    half = WIDTHS[number] // 2
    return ref.at[
        pl.ds(aligned(chip * chip_rows + low, 16), rows),
        pl.ds(aligned(base + core * half + column, 128), columns),
    ]


def gather_kernel(layer, numbers, pieces, *refs):
    count = len(numbers)
    arrays = 3 if 4 in numbers else 2
    take = iter(refs)
    masters = dict(zip(numbers, [next(take) for _ in range(count)]))
    wholes = [next(take) for _ in range(arrays)]
    mine = dict(zip(numbers, [next(take) for _ in range(count)]))
    theirs = dict(zip(numbers, [next(take) for _ in range(count)]))
    blocks = dict(zip(numbers, [next(take) for _ in range(count)]))
    local_sem, pair_send, pair_recv, store_sem, send_sem, recv_sem, core_send, core_recv = take
    spot = place()
    z, y, x, core = spot
    me = chip_number(z, y, x)
    partner = neighbour("core", spot)
    loads = {}
    for number in numbers:
        half = WIDTHS[number] // 2
        loads[number] = pltpu.make_async_copy(
            masters[number].at[0 if number == 4 else layer, :, pl.ds(aligned(core * half, 128), half)],
            mine[number],
            local_sem.at[number],
        )
        loads[number].start()
    greet(spot)
    swaps = []
    for number in numbers:
        half = WIDTHS[number] // 2
        swap = pltpu.make_async_remote_copy(
            src_ref=masters[number].at[0 if number == 4 else layer, :, pl.ds(aligned((1 - core) * half, 128), half)],
            dst_ref=theirs[number],
            send_sem=pair_send.at[number],
            recv_sem=pair_recv.at[number],
            device_id=partner,
            device_id_type=MESH,
        )
        swap.start()
        swaps.append((number, swap))

    def relay(index, away, source, view):
        piece = pieces[index]
        for side in children(piece[8], away):

            def send(side=side):
                pltpu.make_async_remote_copy(
                    src_ref=view,
                    dst_ref=piece_view(wholes[piece[1]], piece, source, core),
                    send_sem=send_sem.at[index, ("up", "down", "x", "y").index(side)],
                    recv_sem=recv_sem.at[index, source],
                    device_id=neighbour(side, spot),
                    device_id_type=MESH,
                ).start()

            guarded(exists(side, z), send)
        pltpu.make_async_remote_copy(
            src_ref=view,
            dst_ref=piece_view(wholes[piece[1]], piece, source, core),
            send_sem=core_send.at[index],
            recv_sem=core_recv.at[index],
            device_id=partner,
            device_id_type=MESH,
        ).start()

    stores = []
    for number, swap in swaps:
        loads[number].wait()
        swap.wait_recv()
        rows = OWN_ROWS[number]
        own, other = mine[number][...], theirs[number][...]
        is_first = core == 0
        block = jnp.concatenate(
            [jnp.where(is_first, own, other), jnp.where(is_first, other, own)], axis=0
        )
        blocks[number][...] = block.astype(jnp.bfloat16)
        for index, piece in enumerate(pieces):
            if piece[0] != number:
                continue
            view = blocks[number].at[pl.ds(piece[4], piece[5]), pl.ds(piece[6], piece[7])]
            store = pltpu.make_async_copy(
                view, piece_view(wholes[piece[1]], piece, me, core), store_sem.at[index]
            )
            store.start()
            stores.append(store)
            relay(index, (0, 0, 0), me, view)
    for away in offsets():
        if away == (0, 0, 0):
            continue
        for index, piece in enumerate(pieces):
            sz, sy, sx, valid = source_of(spot, away)
            source = chip_number(sz, sy, sx)

            def arrival(index=index, piece=piece, source=source):
                view = piece_view(wholes[piece[1]], piece, source, core)
                pltpu.make_async_remote_copy(
                    src_ref=view,
                    dst_ref=view,
                    send_sem=send_sem.at[index, 0],
                    recv_sem=recv_sem.at[index, source],
                    device_id=partner,
                    device_id_type=MESH,
                ).wait_recv()
                relay(index, away, source, view)

            guarded(valid, arrival)
    for store in stores:
        store.wait()
    for _, swap in swaps:
        swap.wait_send()
    for index, piece in enumerate(pieces):
        number, rows, columns = piece[0], piece[5], piece[7]

        def span(chunks, core_at):
            half = WIDTHS[number] // 2
            start = aligned(piece[2] + core_at * half + piece[6], 128)
            return wholes[piece[1]].at[pl.ds(0, chunks * rows), pl.ds(start, columns)]

        def wait_send(chunks, sem):
            pltpu.make_async_remote_copy(
                src_ref=span(chunks, core),
                dst_ref=span(chunks, core),
                send_sem=sem,
                recv_sem=recv_sem.at[index, 0],
                device_id=partner,
                device_id_type=MESH,
            ).wait_send()

        order = piece[8]
        before = 1
        for axis in order:
            if axis == "z":
                for at in range(NZ):

                    @pl.when(z == at)
                    def _(at=at):
                        if at < NZ - 1:
                            wait_send(before * (at + 1), send_sem.at[index, 0])
                        if at > 0:
                            wait_send(before * (NZ - at), send_sem.at[index, 1])

                before *= NZ
            else:
                wait_send(before, send_sem.at[index, 2 if axis == "x" else 3])
                before *= 2
        wait_send(CHIPS, core_send.at[index])
        pltpu.make_async_remote_copy(
            src_ref=span(CHIPS, 1 - core),
            dst_ref=span(CHIPS, 1 - core),
            send_sem=core_send.at[index],
            recv_sem=core_recv.at[index],
            device_id=partner,
            device_id_type=MESH,
        ).wait_recv()


def gather_layer(layer, masters, ident):
    numbers = (4, 0, 1, 2, 3) if len(masters) == 5 else (0, 1, 2, 3)
    pieces = tuple(p for p in PIECES if p[0] in numbers)
    count = len(pieces)
    arrays = 3 if 4 in numbers else 2
    scratch = lambda rows, dtype: [
        pltpu.VMEM((rows * OWN_ROWS[n], WIDTHS[n] // 2), dtype) for n in numbers
    ]
    return pl.pallas_call(
        functools.partial(gather_kernel, layer, numbers, pieces),
        out_shape=tuple(jax.ShapeDtypeStruct(WHOLES[n], jnp.bfloat16) for n in range(arrays)),
        in_specs=[pl.BlockSpec(memory_space=pl.ANY)] * len(numbers),
        out_specs=tuple([pl.BlockSpec(memory_space=pl.ANY)] * arrays),
        scratch_shapes=(
            scratch(1, jnp.float32)
            + scratch(1, jnp.float32)
            + scratch(2, jnp.bfloat16)
            + [
                pltpu.SemaphoreType.DMA((5,)),
                pltpu.SemaphoreType.DMA((5,)),
                pltpu.SemaphoreType.DMA((5,)),
                pltpu.SemaphoreType.DMA((count,)),
                pltpu.SemaphoreType.DMA((count, 4)),
                pltpu.SemaphoreType.DMA((count, CHIPS)),
                pltpu.SemaphoreType.DMA((count,)),
                pltpu.SemaphoreType.DMA((count,)),
            ]
        ),
        name=f"gather_{layer}",
        compiler_params=pltpu.CompilerParams(
            collective_id=ident, has_side_effects=True, vmem_limit_bytes=40 << 20
        ),
        cost_estimate=pl.CostEstimate(flops=0, bytes_accessed=int(2e8), transcendentals=0),
    )(*[masters[n] for n in numbers])


def slot_of(order, side, source):
    sizes = {"z": NZ, "y": NY, "x": NX}
    base = 0
    ahead = 1
    number = 0
    for axis in order:
        at = source[AXIS[axis]]
        for here in ["up", "down"] if axis == "z" else [axis]:
            if axis == "z":
                if here == side:
                    return base + number * NZ + at
                base += ahead * NZ
            else:
                if here == side:
                    return base + number
                base += ahead
        number = number * sizes[axis] + at
        ahead *= sizes[axis]
    return base


def slot_count(order):
    return slot_of(order, None, (0, 0, 0))


def scatter_kernel(numbers, pieces, *refs):
    many = len(numbers)
    count = len(pieces)
    take = iter(refs)
    partials = [next(take) for _ in range(3 if 4 in numbers else 2)]
    named = lambda: dict(zip(numbers, [next(take) for _ in range(many)]))
    outs, own, pair, total, handed = named(), named(), named(), named(), named()
    slots = [next(take) for _ in range(count)]
    base = {p[0]: p[2] for p in pieces}
    array = {p[0]: p[1] for p in pieces}
    (
        own_sem,
        pair_send,
        pair_recv,
        send_sem,
        recv_sem,
        end_send,
        end_recv,
        out_sem,
    ) = take
    spot = place()
    z, y, x, core = spot
    me = chip_number(z, y, x)
    partner = neighbour("core", spot)
    loads = {}
    for number in numbers:
        half = WIDTHS[number] // 2
        load = pltpu.make_async_copy(
            partials[array[number]].at[:, pl.ds(aligned(base[number] + core * half, 128), half)],
            own[number],
            own_sem.at[number],
        )
        load.start()
        loads[number] = load
    greet(spot)
    swaps = {}
    for number in numbers:
        half = WIDTHS[number] // 2
        swap = pltpu.make_async_remote_copy(
            src_ref=partials[array[number]].at[
                :, pl.ds(aligned(base[number] + (1 - core) * half, 128), half)
            ],
            dst_ref=pair[number],
            send_sem=pair_send.at[number],
            recv_sem=pair_recv.at[number],
            device_id=partner,
            device_id_type=MESH,
        )
        swap.start()
        swaps[number] = swap
    ready = set()
    for away in reversed(offsets()):
        for index, piece in enumerate(pieces):
            number, _, _, chip_rows, low, rows, column, columns, order = piece
            if number not in ready:
                ready.add(number)
                loads[number].wait()
                swaps[number].wait_recv()
            sz, sy, sx, valid = source_of(spot, away)
            source = chip_number(sz, sy, sx)
            last = last_axis(order, away)

            def event(
                index=index, number=number, chip_rows=chip_rows, low=low, rows=rows,
                column=column, columns=columns, order=order, source=source, last=last,
                where=(sz, sy, sx),
            ):
                kids = children(order, away)
                for side in kids:

                    def arrived(side=side):
                        slot = slot_of(order, side, where)
                        pltpu.make_async_remote_copy(
                            src_ref=slots[index].at[slot],
                            dst_ref=slots[index].at[slot],
                            send_sem=send_sem.at[index, 0],
                            recv_sem=recv_sem.at[index, slot],
                            device_id=partner,
                            device_id_type=MESH,
                        ).wait_recv()

                    guarded(exists(side, z), arrived)
                view = (pl.ds(aligned(source * chip_rows + low, 16), rows), pl.ds(column, columns))
                value = own[number][view].astype(jnp.float32) + pair[number][view].astype(jnp.float32)
                for side in kids:
                    landed = slots[index][slot_of(order, side, where)].astype(jnp.float32)
                    there = exists(side, z)
                    value = value + (landed if there is None else jnp.where(there, landed, 0.0))
                if last < 0:
                    total[number][pl.ds(low, rows), pl.ds(column, columns)] = value
                    return
                pair[number][view] = value.astype(jnp.bfloat16)
                axis = order[last]
                if axis == "z":
                    side = "up" if away[0] < 0 else "down"
                    parent = neighbour("down" if away[0] < 0 else "up", spot)
                else:
                    side = axis
                    parent = neighbour(axis, spot)
                slot = slot_of(order, side, where)
                pltpu.make_async_remote_copy(
                    src_ref=pair[number].at[view],
                    dst_ref=slots[index].at[slot],
                    send_sem=send_sem.at[index, source],
                    recv_sem=recv_sem.at[index, slot],
                    device_id=parent,
                    device_id_type=MESH,
                ).start()

            guarded(valid, event)
    ends = {}
    for number in numbers:
        rows = OWN_ROWS[number]
        end = pltpu.make_async_remote_copy(
            src_ref=total[number].at[pl.ds(aligned((1 - core) * rows, 8), rows)],
            dst_ref=handed[number],
            send_sem=end_send.at[number],
            recv_sem=end_recv.at[number],
            device_id=partner,
            device_id_type=MESH,
        )
        end.start()
        ends[number] = end
    writes = []
    for number in numbers:
        rows = OWN_ROWS[number]
        half = WIDTHS[number] // 2
        write = pltpu.make_async_copy(
            total[number].at[pl.ds(aligned(core * rows, 8), rows)],
            outs[number].at[:, pl.ds(aligned(core * half, 128), half)],
            out_sem.at[number],
        )
        write.start()
        writes.append(write)
    for number in numbers:
        half = WIDTHS[number] // 2
        ends[number].wait_recv()
        write = pltpu.make_async_copy(
            handed[number],
            outs[number].at[:, pl.ds(aligned((1 - core) * half, 128), half)],
            out_sem.at[5 + number],
        )
        write.start()
        writes.append(write)
    for write in writes:
        write.wait()
    for end in ends.values():
        end.wait_send()
    for swap in swaps.values():
        swap.wait_send()
    for index, piece in enumerate(pieces):
        number, _, _, chip_rows, low, rows, column, columns, order = piece
        for away in offsets():
            if away == (0, 0, 0):
                continue
            sz, sy, sx, valid = source_of(spot, away)
            source = chip_number(sz, sy, sx)

            def sent(index=index, source=source):
                view = (pl.ds(aligned(source * chip_rows + low, 16), rows), pl.ds(column, columns))
                pltpu.make_async_remote_copy(
                    src_ref=pair[number].at[view],
                    dst_ref=slots[index].at[0],
                    send_sem=send_sem.at[index, source],
                    recv_sem=recv_sem.at[index, 0],
                    device_id=partner,
                    device_id_type=MESH,
                ).wait_send()

            guarded(valid, sent)


def scatter_layer(layer, partials, ident):
    numbers = (4, 0, 1, 2, 3) if len(partials) == 3 else (0, 1, 2, 3)
    pieces = tuple(p for p in PIECES if p[0] in numbers)
    count = len(pieces)
    most = max(slot_count(p[8]) for p in pieces)
    scratch = lambda rows, dtype: [
        pltpu.VMEM((rows * OWN_ROWS[n], WIDTHS[n] // 2), dtype) for n in numbers
    ]
    return dict(
        zip(
            numbers,
            pl.pallas_call(
                functools.partial(scatter_kernel, numbers, pieces),
                out_shape=tuple(
                    jax.ShapeDtypeStruct((OWN_ROWS[n], WIDTHS[n]), jnp.float32) for n in numbers
                ),
                in_specs=[pl.BlockSpec(memory_space=pl.ANY)] * len(partials),
                out_specs=tuple([pl.BlockSpec(memory_space=pl.ANY)] * len(numbers)),
                scratch_shapes=(
                    scratch(32, jnp.bfloat16)
                    + scratch(32, jnp.bfloat16)
                    + scratch(2, jnp.float32)
                    + scratch(1, jnp.float32)
                    + [pltpu.VMEM((slot_count(p[8]), p[5], p[7]), jnp.bfloat16) for p in pieces]
                    + [
                        pltpu.SemaphoreType.DMA((5,)),
                        pltpu.SemaphoreType.DMA((5,)),
                        pltpu.SemaphoreType.DMA((5,)),
                        pltpu.SemaphoreType.DMA((count, CHIPS)),
                        pltpu.SemaphoreType.DMA((count, most)),
                        pltpu.SemaphoreType.DMA((5,)),
                        pltpu.SemaphoreType.DMA((5,)),
                        pltpu.SemaphoreType.DMA((10,)),
                    ]
                ),
                name=f"scatter_{layer}",
                compiler_params=pltpu.CompilerParams(
                    collective_id=ident, has_side_effects=True, vmem_limit_bytes=56 << 20
                ),
                cost_estimate=pl.CostEstimate(flops=0, bytes_accessed=int(2e8), transcendentals=0),
            )(*partials),
        )
    )


def passed_along(value, axis, by):
    size = lax.axis_size(axis)
    pairs = [(i, i + by) for i in range(size) if 0 <= i + by < size]
    return lax.ppermute(value, axis, pairs)


def normalize(values):
    centred = values - jnp.mean(values, axis=-1, keepdims=True)
    inverse = lax.rsqrt(jnp.mean(centred * centred, axis=-1, keepdims=True) + EPSILON)
    return (centred * inverse, inverse)


def normalize_back(grad_normed, normed, inverse):
    return inverse * (
        grad_normed
        - jnp.mean(grad_normed, axis=-1, keepdims=True)
        - normed * jnp.mean(grad_normed * normed, axis=-1, keepdims=True)
    )


def rotary_tables(relative):
    indices = jnp.arange(HEAD_DIM // 2).astype(jnp.float32)
    frequency = jnp.exp(indices * (-2.0 * math.log(10000.0) / HEAD_DIM))
    phase = relative.astype(jnp.float32)[:, None] * frequency[None, :]
    cosine, sine = jnp.cos(phase), jnp.sin(phase)
    return (
        jnp.concatenate([cosine] * 4, axis=1),
        jnp.concatenate([-sine, sine, -sine, sine], axis=1),
    )


BAND = 128
VARIANTS = (3, 4, 5, 6, 7, 9)
STEP_COLUMNS = 384
BLOCK = 512
F32 = jnp.float32
BF16 = jnp.bfloat16
MATMUL = (((1,), (0,)), ((), ()))
MATMUL_RIGHT = (((1,), (1,)), ((), ()))
MATMUL_LEFT = (((0,), (0,)), ((), ()))


def product(left, right, dims=MATMUL):
    return lax.dot_general(left, right, dims, preferred_element_type=F32)


def vmem(limit=56):
    return pltpu.CompilerParams(vmem_limit_bytes=limit << 20)


def cost(flops, moved):
    return pl.CostEstimate(flops=int(flops), bytes_accessed=int(moved), transcendentals=0)


def swap_halves(values):
    lane = lax.broadcasted_iota(jnp.int32, values.shape, 1)
    low = lax.rem(lane, HEAD_DIM) < HEAD_DIM // 2
    return jnp.where(
        low,
        pltpu.roll(values, 2 * HEAD_DIM - HEAD_DIM // 2, 1),
        pltpu.roll(values, HEAD_DIM // 2, 1),
    )


def turn(values, cosine, sine):
    parts = []
    for at in range(0, values.shape[1], 128):
        part = values[:, at : at + 128]
        parts.append(part * cosine + swap_halves(part) * sine)
    return jnp.concatenate(parts, axis=1)


def project_kernel(x_ref, w_ref, bias_ref, mod_ref, cos_ref, sin_ref, q_ref, kv_ref, h_ref):
    step = pl.program_id(0)

    @pl.when(step == 0)
    def _():
        normed, _ = normalize(x_ref[...].astype(F32))
        h_ref[...] = (normed * (1.0 + mod_ref[1:2]) + mod_ref[0:1]).astype(BF16)

    y = product(h_ref[...], w_ref[...]) + bias_ref[...]

    @pl.when(step < 2)
    def _():
        q_ref[...] = turn(y, cos_ref[...], sin_ref[...]).astype(BF16)

    @pl.when((step >= 2) & (step < 4))
    def _():
        kv_ref[0] = turn(y, cos_ref[...], sin_ref[...]).astype(BF16)

    @pl.when(step >= 4)
    def _():
        kv_ref[0] = y.astype(BF16)


def project(stream, square, bias, modulation, cosine, sine):
    rows = stream.shape[0]
    whole = lambda shape: pl.BlockSpec(shape, lambda c: (0,) * len(shape))
    return pl.pallas_call(
        project_kernel,
        grid=(6,),
        in_specs=[
            whole((rows, D)),
            pl.BlockSpec((D, STEP_COLUMNS), lambda c: (0, c)),
            pl.BlockSpec((1, STEP_COLUMNS), lambda c: (0, c)),
            whole((4, D)),
            whole((rows, 128)),
            whole((rows, 128)),
        ],
        out_specs=(
            pl.BlockSpec((rows, STEP_COLUMNS), lambda c: (0, jnp.minimum(c, 1))),
            pl.BlockSpec(
                (1, rows, STEP_COLUMNS),
                lambda c: (jnp.maximum(c - 2, 0) // 2, 0, jnp.maximum(c - 2, 0) % 2),
            ),
            whole((rows, D)),
        ),
        out_shape=(
            jax.ShapeDtypeStruct((rows, D), BF16),
            jax.ShapeDtypeStruct((2, rows, D), BF16),
            jax.ShapeDtypeStruct((rows, D), BF16),
        ),
        compiler_params=vmem(),
        cost_estimate=cost(2 * rows * D * 3 * D, 8e6),
        name="project",
    )(stream, square, bias, modulation, cosine, sine)


def stack_heads(pair):
    lane = lax.broadcasted_iota(jnp.int32, pair.shape, 1)
    zero = jnp.zeros_like(pair)
    return jnp.concatenate(
        [jnp.where(lane < HEAD_DIM, pair, zero), jnp.where(lane < HEAD_DIM, zero, pair)], axis=0
    )


def merge_heads(stacked):
    rows = stacked.shape[0] // 2
    lane = lax.broadcasted_iota(jnp.int32, (rows, stacked.shape[1]), 1)
    return jnp.where(lane < HEAD_DIM, stacked[:rows], stacked[rows:])


def over_bands(bounds_ref, count, action):
    def one(number, carry):
        low, need = bounds_ref[0, number], bounds_ref[1, number]
        before = 0
        for size in VARIANTS:

            @pl.when((need > before) & (need <= size))
            def _(size=size):
                start = jnp.minimum(low, count - size) * BAND
                action(pl.multiple_of(number * BAND, BAND), pl.multiple_of(start, BAND), size * BAND)

            before = size
        return carry

    lax.fori_loop(0, bounds_ref.shape[1], one, 0)


def attend_kernel(bounds_ref, q_ref, low_ref, own_ref, high_ref, idq_ref, idk_ref, o_ref, lse_ref, ext):
    rows = own_ref.shape[1]
    for at in range(2):
        ext[at, :WIN_MAX] = low_ref[at]
        ext[at, WIN_MAX : WIN_MAX + rows] = own_ref[at]
        ext[at, WIN_MAX + rows :] = high_ref[at]

    def block(first, start, size):
        mine = pl.ds(first, BAND)
        queries = stack_heads(q_ref[mine, :]) * jnp.asarray(HEAD_DIM**-0.5, BF16)
        keys = ext[0, pl.ds(start, size), :]
        scores = product(queries, keys, MATMUL_RIGHT)
        ids = idq_ref[mine, :]
        allowed = jnp.concatenate([ids] * (size // BAND), axis=1) == idk_ref[0:1, pl.ds(start, size)]
        scores = jnp.where(jnp.concatenate([allowed, allowed], axis=0), scores, NEGATIVE)
        peak = jnp.max(scores, axis=1, keepdims=True)
        weights = jnp.exp(scores - peak)
        total = jnp.sum(weights, axis=1, keepdims=True)
        values = ext[1, pl.ds(start, size), :]
        mixed = product(weights.astype(BF16), values) * (1.0 / total)
        o_ref[mine, :] = merge_heads(mixed).astype(BF16)
        wide = jnp.broadcast_to(peak + jnp.log(total), (2 * BAND, BAND))
        lse_ref[0, 0:1, mine] = wide[:BAND].T[0:1]
        lse_ref[0, 1:2, mine] = wide[BAND:].T[0:1]

    over_bands(bounds_ref, (rows + 2 * WIN_MAX) // BAND, block)


def pair_spec(rows):
    return pl.BlockSpec((2, rows, 128), lambda j, b: (0, 0, j))


def attend(bounds, queries, low, own, high, ids_query, ids_key):
    rows = queries.shape[0]
    wide = rows + 2 * WIN_MAX
    column = pl.BlockSpec((rows, 128), lambda j, b: (0, j))
    return pl.pallas_call(
        attend_kernel,
        grid_spec=pltpu.PrefetchScalarGridSpec(
            num_scalar_prefetch=1,
            grid=(HEADS // 2,),
            in_specs=[
                column,
                pair_spec(WIN_MAX),
                pair_spec(rows),
                pair_spec(WIN_MAX),
                pl.BlockSpec((rows, 128), lambda j, b: (0, 0)),
                pl.BlockSpec((8, wide), lambda j, b: (0, 0)),
            ],
            out_specs=(column, pl.BlockSpec((1, 8, rows), lambda j, b: (j, 0, 0))),
            scratch_shapes=[pltpu.VMEM((2, wide, 128), BF16)],
        ),
        out_shape=(
            jax.ShapeDtypeStruct((rows, D), BF16),
            jax.ShapeDtypeStruct((HEADS // 2, 8, rows), F32),
        ),
        compiler_params=vmem(),
        cost_estimate=cost(5e9, 8e6),
        name="attend",
    )(bounds, queries, low, own, high, ids_query, ids_key)


def attend_back_kernel(
    bounds_ref, q_ref, g_ref, o_ref, lse_ref, low_ref, own_ref, high_ref, idq_ref, idk_ref,
    cos_ref, sin_ref, dq_ref, dlow_ref, down_ref, dhigh_ref, ext, dext,
):
    rows = own_ref.shape[1]
    for at in range(2):
        ext[at, :WIN_MAX] = low_ref[at]
        ext[at, WIN_MAX : WIN_MAX + rows] = own_ref[at]
        ext[at, WIN_MAX + rows :] = high_ref[at]
    dext[...] = jnp.zeros_like(dext)

    def block(first, start, size):
        mine = pl.ds(first, BAND)
        band = pl.ds(start, size)
        queries = stack_heads(q_ref[mine, :]) * jnp.asarray(HEAD_DIM**-0.5, BF16)
        grads = stack_heads(g_ref[mine, :])
        keys = ext[0, band, :]
        scores = product(keys, queries, MATMUL_RIGHT)
        ids = idk_ref[band, :] == idq_ref[0:1, mine]
        allowed = jnp.concatenate([ids, ids], axis=1)
        lse = jnp.concatenate([lse_ref[0, 0:1, mine], lse_ref[0, 1:2, mine]], axis=1)
        weights = jnp.where(allowed, jnp.exp(scores - lse), 0.0)
        both_heads = (g_ref[mine, :].astype(F32) * o_ref[mine, :].astype(F32)).T
        delta = jnp.concatenate(
            [
                jnp.sum(both_heads[:HEAD_DIM], axis=0, keepdims=True),
                jnp.sum(both_heads[HEAD_DIM:], axis=0, keepdims=True),
            ],
            axis=1,
        )
        values = ext[1, band, :]
        grad_weights = product(values, grads, MATMUL_RIGHT)
        grad_scores = (weights * (grad_weights - delta)).astype(BF16)
        dext[0, band, :] += product(grad_scores, queries)
        dext[1, band, :] += product(weights.astype(BF16), grads)
        grad_queries = merge_heads(product(grad_scores, keys, MATMUL_LEFT)) * HEAD_DIM**-0.5
        dq_ref[mine, :] = turn(grad_queries, cos_ref[mine, :], -sin_ref[mine, :]).astype(BF16)

    over_bands(bounds_ref, (rows + 2 * WIN_MAX) // BAND, block)
    dlow_ref[...] = dext[:, :WIN_MAX].astype(BF16)
    down_ref[...] = dext[:, WIN_MAX : WIN_MAX + rows]
    dhigh_ref[...] = dext[:, WIN_MAX + rows :].astype(BF16)


def attend_back(bounds, queries, grads, attended, lse, low, own, high, ids_query, ids_key, cosine, sine):
    rows = queries.shape[0]
    wide = rows + 2 * WIN_MAX
    column = pl.BlockSpec((rows, 128), lambda j, b: (0, j))
    fixed = lambda shape: pl.BlockSpec(shape, lambda j, b: (0,) * len(shape))
    return pl.pallas_call(
        attend_back_kernel,
        grid_spec=pltpu.PrefetchScalarGridSpec(
            num_scalar_prefetch=1,
            grid=(HEADS // 2,),
            in_specs=[
                column,
                column,
                column,
                pl.BlockSpec((1, 8, rows), lambda j, b: (j, 0, 0)),
                pair_spec(WIN_MAX),
                pair_spec(rows),
                pair_spec(WIN_MAX),
                fixed((8, rows)),
                fixed((wide, 128)),
                fixed((rows, 128)),
                fixed((rows, 128)),
            ],
            out_specs=(column, pair_spec(WIN_MAX), pair_spec(rows), pair_spec(WIN_MAX)),
            scratch_shapes=[pltpu.VMEM((2, wide, 128), BF16), pltpu.VMEM((2, wide, 128), F32)],
        ),
        out_shape=(
            jax.ShapeDtypeStruct((rows, D), BF16),
            jax.ShapeDtypeStruct((2, WIN_MAX, D), BF16),
            jax.ShapeDtypeStruct((2, rows, D), F32),
            jax.ShapeDtypeStruct((2, WIN_MAX, D), BF16),
        ),
        compiler_params=vmem(),
        cost_estimate=cost(12e9, 16e6),
        name="attend_back",
    )(bounds, queries, grads, attended, lse, low, own, high, ids_query, ids_key, cosine, sine)


def feed_kernel(
    o_ref, x_ref, wo_ref, we_ref, ws_ref, bo_ref, be_ref, bs_ref, mod_ref,
    mid_ref, h_ref, z_ref, slope_ref, out_ref,
):
    step = pl.program_id(0)

    @pl.when(step == 0)
    def _():
        middle = x_ref[...].astype(F32) + (product(o_ref[...], wo_ref[...]) + bo_ref[...])
        mid_ref[...] = middle
        normed, _ = normalize(middle)
        h_ref[...] = (normed * (1.0 + mod_ref[3:4]) + mod_ref[2:3]).astype(BF16)
        out_ref[...] = middle + bs_ref[...]

    u = product(h_ref[...], we_ref[...]) + be_ref[...]
    share = 0.5 + 0.5 * lax.erf(u * (0.5**0.5))
    active = (u * share).astype(BF16)
    z_ref[...] = active
    slope_ref[...] = (share + u * (jnp.exp(-0.5 * u * u) * (2.0 * math.pi) ** -0.5)).astype(BF16)
    out_ref[...] += product(active, ws_ref[...])


def feed(attended, stream, square, shrink, bias, modulation):
    rows = stream.shape[0]
    whole = lambda shape: pl.BlockSpec(shape, lambda c: (0,) * len(shape))
    width = STEP_COLUMNS
    return pl.pallas_call(
        feed_kernel,
        grid=(FF // width,),
        in_specs=[
            whole((rows, D)),
            whole((rows, D)),
            pl.BlockSpec((D, D), lambda c: (0, 3)),
            pl.BlockSpec((D, width), lambda c: (0, 4 * D // width + c)),
            pl.BlockSpec((width, D), lambda c: (c, 0)),
            pl.BlockSpec((1, D), lambda c: (0, 3)),
            pl.BlockSpec((1, width), lambda c: (0, 4 * D // width + c)),
            pl.BlockSpec((1, D), lambda c: (0, 8)),
            whole((4, D)),
        ],
        out_specs=(
            whole((rows, D)),
            whole((rows, D)),
            pl.BlockSpec((rows, width), lambda c: (0, c)),
            pl.BlockSpec((rows, width), lambda c: (0, c)),
            whole((rows, D)),
        ),
        out_shape=(
            jax.ShapeDtypeStruct((rows, D), F32),
            jax.ShapeDtypeStruct((rows, D), BF16),
            jax.ShapeDtypeStruct((rows, FF), BF16),
            jax.ShapeDtypeStruct((rows, FF), BF16),
            jax.ShapeDtypeStruct((rows, D), F32),
        ),
        compiler_params=vmem(),
        cost_estimate=cost(2 * rows * D * (D + 2 * FF), 24e6),
        name="feed",
    )(attended, stream, square, square, shrink, bias, bias, bias, modulation)


def feed_back_kernel(
    g_ref, z_ref, slope_ref, h_ref, mid_ref, o_ref, we_ref, ws_ref, wo_ref, mod_ref,
    square_ref, dshr_ref, mid_grad_ref, do_ref, dbe_ref, sums_ref,
    low, turned, total,
):
    step = pl.program_id(0)
    chunks = FF // STEP_COLUMNS

    @pl.when(step == 0)
    def _():
        low[...] = g_ref[...].astype(BF16)
        turned[...] = h_ref[...].T
        total[...] = jnp.zeros_like(total)
        sums_ref[3:4] = jnp.sum(low[...].astype(F32), axis=0, keepdims=True)

    @pl.when(step < chunks)
    def _():
        grad_active = product(low[...], ws_ref[...], MATMUL_RIGHT)
        grad_hidden = (grad_active * slope_ref[...].astype(F32)).astype(BF16)
        dbe_ref[...] = jnp.sum(grad_hidden.astype(F32), axis=0, keepdims=True)
        dshr_ref[...] = product(z_ref[...], low[...], MATMUL_LEFT).astype(BF16)
        square_ref[...] = product(turned[...], grad_hidden).astype(BF16)
        total[...] += product(grad_hidden, we_ref[...], MATMUL_RIGHT)

    @pl.when(step == chunks)
    def _():
        normed, inverse = normalize(mid_ref[...])
        grad = total[...]
        sums_ref[0:1] = jnp.sum(grad, axis=0, keepdims=True)
        sums_ref[1:2] = jnp.sum(grad * normed, axis=0, keepdims=True)
        middle = g_ref[...].astype(F32) + normalize_back(grad * (1.0 + mod_ref[3:4]), normed, inverse)
        mid_grad_ref[...] = middle
        low[...] = middle.astype(BF16)
        sums_ref[2:3] = jnp.sum(low[...].astype(F32), axis=0, keepdims=True)
        do_ref[...] = product(low[...], wo_ref[...], MATMUL_RIGHT).astype(BF16)
        turned[...] = o_ref[...].T
        square_ref[...] = product(turned[...], low[:, :STEP_COLUMNS]).astype(BF16)

    @pl.when(step == chunks + 1)
    def _():
        square_ref[...] = product(turned[...], low[:, STEP_COLUMNS:]).astype(BF16)


def feed_back(grad, active, slope, hidden_in, middle, attended, square, shrink, modulation):
    rows = grad.shape[0]
    whole = lambda shape: pl.BlockSpec(shape, lambda c: (0,) * len(shape))
    width = STEP_COLUMNS
    chunks = FF // width
    upto = lambda c: jnp.minimum(c, chunks - 1)
    return pl.pallas_call(
        feed_back_kernel,
        grid=(chunks + 2,),
        in_specs=[
            whole((rows, D)),
            pl.BlockSpec((rows, width), lambda c: (0, upto(c))),
            pl.BlockSpec((rows, width), lambda c: (0, upto(c))),
            whole((rows, D)),
            whole((rows, D)),
            whole((rows, D)),
            pl.BlockSpec((D, width), lambda c: (0, 4 * D // width + upto(c))),
            pl.BlockSpec((width, D), lambda c: (upto(c), 0)),
            pl.BlockSpec((D, D), lambda c: (0, 3)),
            whole((4, D)),
        ],
        out_specs=(
            pl.BlockSpec(
                (D, width),
                lambda c: (0, jnp.where(c < chunks, 4 * D // width + c, 3 * D // width + c - chunks)),
            ),
            pl.BlockSpec((width, D), lambda c: (upto(c), 0)),
            whole((rows, D)),
            whole((rows, D)),
            pl.BlockSpec((1, width), lambda c: (0, upto(c))),
            whole((4, D)),
        ),
        out_shape=(
            jax.ShapeDtypeStruct((D, 4 * D + FF), BF16),
            jax.ShapeDtypeStruct((FF, D), BF16),
            jax.ShapeDtypeStruct((rows, D), F32),
            jax.ShapeDtypeStruct((rows, D), BF16),
            jax.ShapeDtypeStruct((1, FF), F32),
            jax.ShapeDtypeStruct((4, D), F32),
        ),
        scratch_shapes=[
            pltpu.VMEM((rows, D), BF16),
            pltpu.VMEM((D, rows), BF16),
            pltpu.VMEM((rows, D), F32),
        ],
        compiler_params=vmem(),
        cost_estimate=cost(4 * rows * D * (D + 2 * FF), 40e6),
        name="feed_back",
    )(grad, active, slope, hidden_in, middle, attended, square, shrink, square, modulation)


def project_back_kernel(
    dq_ref, own_ref, below_ref, above_ref, cos_ref, sin_ref, h_ref, x_ref, mid_grad_ref, w_ref, mod_ref,
    square_in, square_ref, out_ref, db_ref, sums_ref, turned, total,
):
    step = pl.program_id(0)

    @pl.when(step == 0)
    def _():
        turned[...] = h_ref[...].T
        total[...] = jnp.zeros_like(total)

    def chunk(grad):
        db_ref[...] = jnp.sum(grad.astype(F32), axis=0, keepdims=True)
        square_ref[...] = product(turned[...], grad).astype(BF16)
        total[...] += product(grad, w_ref[...], MATMUL_RIGHT)

    def summed():
        return own_ref[0] + below_ref[0].astype(F32) + above_ref[0].astype(F32)

    @pl.when(step < 2)
    def _():
        chunk(dq_ref[...])

    @pl.when((step >= 2) & (step < 4))
    def _():
        chunk(turn(summed(), cos_ref[...], -sin_ref[...]).astype(BF16))

    @pl.when(step >= 4)
    def _():
        chunk(summed().astype(BF16))

    @pl.when(step == 5)
    def _():
        normed, inverse = normalize(x_ref[...].astype(F32))
        grad = total[...]
        sums_ref[0:1] = jnp.sum(grad, axis=0, keepdims=True)
        sums_ref[1:2] = jnp.sum(grad * normed, axis=0, keepdims=True)
        out_ref[...] = mid_grad_ref[...] + normalize_back(
            grad * (1.0 + mod_ref[1:2]), normed, inverse
        )


def project_back(dq, own, below, above, cosine, sine, hidden_in, stream, mid_grad, square, modulation, square_grad):
    rows = dq.shape[0]
    width = STEP_COLUMNS
    whole = lambda shape: pl.BlockSpec(shape, lambda c: (0,) * len(shape))
    later = pl.BlockSpec(
        (1, rows, width), lambda c: (jnp.maximum(c - 2, 0) // 2, 0, jnp.maximum(c - 2, 0) % 2)
    )
    return pl.pallas_call(
        project_back_kernel,
        grid=(6,),
        in_specs=[
            pl.BlockSpec((rows, width), lambda c: (0, jnp.minimum(c, 1))),
            later,
            later,
            later,
            whole((rows, 128)),
            whole((rows, 128)),
            whole((rows, D)),
            whole((rows, D)),
            whole((rows, D)),
            pl.BlockSpec((D, width), lambda c: (0, c)),
            whole((4, D)),
            pl.BlockSpec(memory_space=pl.ANY),
        ],
        out_specs=(
            pl.BlockSpec((D, width), lambda c: (0, c)),
            whole((rows, D)),
            pl.BlockSpec((1, width), lambda c: (0, c)),
            whole((2, D)),
        ),
        out_shape=(
            jax.ShapeDtypeStruct((D, 4 * D + FF), BF16),
            jax.ShapeDtypeStruct((rows, D), F32),
            jax.ShapeDtypeStruct((1, 3 * D), F32),
            jax.ShapeDtypeStruct((2, D), F32),
        ),
        scratch_shapes=[pltpu.VMEM((D, rows), BF16), pltpu.VMEM((rows, D), F32)],
        input_output_aliases={11: 0},
        compiler_params=vmem(),
        cost_estimate=cost(4 * rows * D * 3 * D, 20e6),
        name="project_back",
    )(dq, own, below, above, cosine, sine, hidden_in, stream, mid_grad, square, modulation, square_grad)


def direct():
    return lax.axis_size("dp") == NZ * NY and lax.axis_size("fsdp") == NX * 2


BOTH = ("dp", "fsdp")


def pack_small(bias, table):
    flat = jnp.concatenate([bias.reshape(-1), table.reshape(-1)])
    flat = jnp.pad(flat, (0, OWN_ROWS[4] * SMALL - flat.shape[0]))
    return flat.reshape(1, OWN_ROWS[4], SMALL)


def unpack_small(whole, lead_row):
    count = lax.axis_size("dp") * lax.axis_size("fsdp")
    flat = whole.reshape(count, -1).astype(F32)
    wide = LAYERS * 9 * D // count
    bias = flat[:, :wide].reshape(count, LAYERS, 9, -1).transpose(1, 2, 0, 3).reshape(LAYERS, 9 * D)
    table = flat[:, wide : wide + LAYERS * LEADS * 4 * D // count].reshape(count, LAYERS, LEADS, -1)
    rows = lax.dynamic_index_in_dim(table, lead_row, 2, keepdims=False)
    return bias, rows.transpose(1, 0, 2).reshape(LAYERS, 4, D)


def plain_fetch(masters, layer):
    square = jnp.concatenate([masters[n][layer].astype(BF16) for n in range(3)], axis=1)
    shrink = masters[3][layer].astype(BF16)
    return (
        lax.all_gather(square, BOTH, axis=0, tiled=True),
        lax.all_gather(shrink, BOTH, axis=0, tiled=True),
    )


def fetch_layers(masters, lead_row):
    if direct():
        small = pack_small(masters[4], masters[5])
        *first, whole = gather_layer(0, (*masters[:4], small), 0)
        bias, modulation = unpack_small(whole, lead_row)
        layers = [tuple(first)]
    else:
        bias = lax.all_gather(masters[4].astype(BF16), BOTH, axis=2, tiled=True)
        bias = bias.astype(F32).reshape(LAYERS, 9 * D)
        table = lax.all_gather(masters[5].astype(BF16), BOTH, axis=2, tiled=True)
        modulation = lax.dynamic_index_in_dim(table, lead_row, 1, keepdims=False)
        modulation = modulation.astype(F32).reshape(LAYERS, 4, D)
        layers = [plain_fetch(masters, 0)]
    for layer in range(1, LAYERS):
        if direct() and not LATER_OFFLOADED:
            layers.append(tuple(gather_layer(layer, masters[:4], layer)))
        else:
            layers.append(plain_fetch(masters, layer))
    return layers, bias, modulation


def plain_reduce(square, shrink):
    square = lax.psum_scatter(square, BOTH, scatter_dimension=0, tiled=True).astype(F32)
    shrink = lax.psum_scatter(shrink, BOTH, scatter_dimension=0, tiled=True).astype(F32)
    return [square[:, : 3 * D], square[:, 3 * D : 4 * D], square[:, 4 * D :], shrink]


def reduce_small_inputs(bias_grads, rows_grads, lead_hot):
    count = lax.axis_size("dp") * lax.axis_size("fsdp")
    bias = bias_grads.reshape(LAYERS * 9, count, -1).transpose(1, 0, 2).reshape(count, -1)
    rows = rows_grads.reshape(LAYERS, 1, count, -1) * lead_hot[None, :, None, None]
    rows = rows.transpose(2, 0, 1, 3).reshape(count, -1)
    flat = jnp.concatenate([bias, rows], axis=1)
    used = flat.shape[1]
    flat = jnp.pad(flat, ((0, 0), (0, OWN_ROWS[4] * SMALL - used)))
    return flat.reshape(-1, SMALL).astype(BF16)


def split_small(own):
    count = lax.axis_size("dp") * lax.axis_size("fsdp")
    flat = own.reshape(-1)
    wide = LAYERS * 9 * D // count
    used = wide + LAYERS * LEADS * 4 * D // count
    return flat[:wide].reshape(LAYERS, 9, -1), flat[wide:used].reshape(LAYERS, LEADS, -1)


def bands(segment_ids, segment_starts, padding_mask, offset, rows):
    length = segment_ids.shape[0]
    position = jnp.arange(length, dtype=jnp.int32)
    real = padding_mask == 1
    names = jnp.where(real, segment_ids, length + position)
    fill = jnp.full((WIN_MAX,), -1, jnp.int32)
    wide = lax.dynamic_slice_in_dim(
        jnp.concatenate([fill, names, fill - 1]), offset, rows + 2 * WIN_MAX
    )
    own = lax.dynamic_slice_in_dim(names, offset, rows)
    at = offset + jnp.arange(rows // BAND, dtype=jnp.int32) * BAND
    last = at + BAND - 1
    begins = jnp.where(real, segment_starts, position)[at]
    ends = jnp.sum((segment_ids[None, :] <= segment_ids[last][:, None]).astype(jnp.int32), axis=1)
    ends = jnp.where(real[last], ends, last + 1)
    low = (begins - offset + WIN_MAX) // BAND
    need = (ends - offset + WIN_MAX + BAND - 1) // BAND - low
    return jnp.stack([low, need]), own, wide


def exchange(pair):
    return passed_along(pair, "fsdp", 1), pair, passed_along(pair, "fsdp", -1)


def adam_update(weight, gradient, moment, square, step_rate, decay_rate):
    moment = BETA_ONE * moment + (1.0 - BETA_ONE) * gradient
    square = BETA_TWO * square + (1.0 - BETA_TWO) * gradient * gradient
    first_fix = 1.0 - BETA_ONE**STEP
    second_fix = 1.0 - BETA_TWO**STEP
    update = moment / first_fix / (jnp.sqrt(square / second_fix) + ADAM_EPSILON)
    weight = weight - step_rate * (update + decay_rate * weight)
    return (weight, moment, square, weight.astype(jnp.bfloat16))


def shards(
    tokens,
    cotangent,
    segment_ids,
    segment_starts,
    padding_mask,
    lead_index,
    input_weights,
    input_moment,
    input_square,
    output_weights,
    output_moment,
    output_square,
    expand_weights,
    expand_moment,
    expand_square,
    shrink_weights,
    shrink_moment,
    shrink_square,
    bias_vector,
    bias_moment,
    bias_square,
    lead_table,
    lead_moment,
    lead_square,
):
    rows = tokens.shape[0]
    offset = lax.axis_index("fsdp") * rows
    bounds, own_names, wide_names = bands(segment_ids, segment_starts, padding_mask, offset, rows)
    ids_query = jnp.broadcast_to(own_names[:, None], (rows, 128))
    ids_key = jnp.broadcast_to(wide_names[None, :], (8, wide_names.shape[0]))
    ids_query_row = jnp.broadcast_to(own_names[None, :], (8, rows))
    ids_key_column = jnp.broadcast_to(wide_names[:, None], (wide_names.shape[0], 128))
    own_starts = lax.dynamic_slice_in_dim(segment_starts, offset, rows)
    relative = offset + jnp.arange(rows, dtype=jnp.int32) - own_starts
    cosine, sine = rotary_tables(relative)
    lead_row = lead_index[0]
    lead_hot = (jnp.arange(LEADS, dtype=jnp.int32) == lead_row).astype(F32)
    masters = (input_weights, output_weights, expand_weights, shrink_weights, bias_vector, lead_table)
    layers, bias, modulation = fetch_layers(masters, lead_row)
    stream = tokens
    saved = []
    for layer in range(LAYERS):
        square, shrink = layers[layer]
        own_bias, own_mod = bias[layer][None], modulation[layer]
        queries, pair, first_in = project(stream, square, own_bias, own_mod, cosine, sine)
        low, own, high = exchange(pair)
        attended, lse = attend(bounds, queries, low, own, high, ids_query, ids_key)
        middle, second_in, active, slope, result = feed(
            attended, stream, square, shrink, own_bias, own_mod
        )
        saved.append(
            (stream, queries, low, own, high, first_in, attended, lse, middle, second_in, active, slope)
        )
        stream = result
    grad = cotangent
    reduced = [None] * LAYERS
    bias_grads = [None] * LAYERS
    rows_grads = [None] * LAYERS
    for layer in reversed(range(LAYERS)):
        square, shrink = layers[layer]
        own_mod = modulation[layer]
        before, queries, low, own, high, first_in, attended, lse, middle, second_in, active, slope = saved[
            layer
        ]
        square_grad, shrink_grad, mid_grad, attended_grad, expand_bias, sums = feed_back(
            grad, active, slope, second_in, middle, attended, square, shrink, own_mod
        )
        dq, to_below, own_grad, to_above = attend_back(
            bounds, queries, attended_grad, attended, lse, low, own, high, ids_query_row,
            ids_key_column, cosine, sine,
        )
        below = passed_along(to_above, "fsdp", 1)
        above = passed_along(to_below, "fsdp", -1)
        square_grad, grad, input_bias, more = project_back(
            dq, own_grad, below, above, cosine, sine, first_in, before, mid_grad, square, own_mod,
            square_grad,
        )
        bias_grads[layer] = jnp.concatenate([input_bias[0], sums[2], expand_bias[0], sums[3]])
        rows_grads[layer] = jnp.concatenate([more[0], more[1], sums[0], sums[1]])
        if direct() and layer == 0:
            small = reduce_small_inputs(jnp.stack(bias_grads), jnp.stack(rows_grads), lead_hot)
            summed = scatter_layer(layer, (square_grad, shrink_grad, small), LAYERS + layer)
            reduced[layer] = [summed[n] for n in range(4)]
            bias_grad, lead_grad = split_small(summed[4])
        elif direct() and not LATER_OFFLOADED:
            summed = scatter_layer(layer, (square_grad, shrink_grad), LAYERS + layer)
            reduced[layer] = [summed[n] for n in range(4)]
        else:
            reduced[layer] = plain_reduce(square_grad, shrink_grad)
    if not direct():
        bias_grad = lax.psum_scatter(
            jnp.stack(bias_grads).reshape(LAYERS, 9, D), BOTH, scatter_dimension=2, tiled=True
        )
        lead_grad = lax.psum_scatter(
            jnp.stack(rows_grads)[:, None, :] * lead_hot[None, :, None], BOTH, scatter_dimension=2,
            tiled=True,
        )
    moments = (input_moment, output_moment, expand_moment, shrink_moment, bias_moment, lead_moment)
    squares = (input_square, output_square, expand_square, shrink_square, bias_square, lead_square)
    results = []
    for number in range(6):
        if number < 4:
            gradient = jnp.stack([reduced[layer][number] for layer in range(LAYERS)])
        else:
            gradient = (bias_grad, lead_grad)[number - 4]
        results.append(
            adam_update(
                masters[number],
                gradient,
                moments[number],
                squares[number],
                RATE_MATRIX if number < 4 else RATE_VECTOR,
                DECAY if number < 4 else 0.0,
            )
        )
    return (stream, grad, *(array for four in results for array in four))


def solution(mesh):
    rows = P(("dp", "fsdp"), None)
    matrix = P(None, ("dp", "fsdp"), None)
    vector = P(None, None, ("dp", "fsdp"))
    return jax.shard_map(
        shards,
        mesh=mesh,
        in_specs=(rows,) * 2 + (P("dp"),) * 4 + (matrix,) * 12 + (vector,) * 6,
        out_specs=(rows,) * 2 + (matrix,) * 16 + (vector,) * 8,
        check_vma=False,
    )
```

time: 926 us -> 574 us (0.62); the launches traced: 908 us -> 569 us
  matrix products: 320 us -> 0 us
  other arithmetic: 146 us -> 13 us
  Pallas kernels: 295 us -> 391 us
  local copies, waits for them, and re-layouts: 98.1 us -> 26.7 us
  waiting for transfers between devices: 0.34 us -> 43.3 us
  starting transfers between devices: 45.2 us -> 79.9 us
  between operations: 3.95 us -> 15.8 us
    dot_general x36 -> x0, matrix products: 320 us -> none  [the longest x2 57.8 us: attend_backward(): jnp.einsum('qhd,khd->hqk', grad_attended, value_block, preferred_element_...]
    pallas_call x4 -> x14, Pallas kernels: 295 us -> 391 us  [the longest x1 99.4 us: scatter_layer(): pl.pallas_call(functools.partial(scatter_kernel, numbers, pieces), out_sh...]
    convert_element_type x7 -> x2, other arithmetic: 48.8 us -> 1 us  [the longest x1 1 us: plain_reduce(): lax.psum_scatter(square, BOTH, scatter_dimension=0, tiled=True).astype(F32)]
    ppermute x4 -> x8, starting transfers between devices: 34.2 us -> 79.5 us  [passed_along(): return lax.ppermute(value, axis, pairs)]
    slice x43 -> x17, local copies, waits for them, and re-layouts: 48.9 us -> 3.62 us  [the longest x6 1.74 us: shards(): own_bias, own_mod = (bias[layer][None], modulation[layer])]
    reduce_sum x11 -> x1, other arithmetic: 43 us -> 0.2 us  [bands(): jnp.sum((segment_ids[None, :] <= segment_ids[last][:, None]).astype(jnp.i...]
    reduce_scatter x0 -> x2, waiting for transfers between devices: none -> 28.1 us  [the longest x1 28.1 us: plain_reduce(): lax.psum_scatter(square, BOTH, scatter_dimension=0, tiled=True).astype(F32)]
    unnamed x323 -> x86, local copies, waits for them, and re-layouts: 32.8 us -> 10.4 us
  transfers between devices with their start and end apart: 8 -> 12, of which waited for: 1 -> 7; matrix products, arithmetic and copies ran while one was open for 4% -> 5% of each run, Pallas kernels for 8% -> 62%
where the time goes in v2:
time: 574 us; the launch traced here: 569 us
  Pallas kernels  391 us (68%)
  starting transfers between devices  79.9 us (14%)
  waiting for transfers between devices  43.3 us (8%)
  local copies, waits for them, and re-layouts  26.7 us (5%)
  between operations  15.8 us (3%)
  other arithmetic  13 us (2%)
    pallas_call x1, Pallas kernels, scatter_layer(): pl.pallas_call(functools.partial(scatter_kernel, numbers, pieces), out_sh...  99.4 us
    pallas_call x1, Pallas kernels, gather_layer(): pl.pallas_call(functools.partial(gather_kernel, layer, numbers, pieces),...  92.6 us
    ppermute x8, starting transfers between devices, passed_along(): return lax.ppermute(value, axis, pairs)  79.5 us
    pallas_call x2, Pallas kernels, feed_back(): pl.pallas_call(feed_back_kernel, grid=(chunks + 2,), in_specs=[whole((row...  46.7 us
    pallas_call x2, Pallas kernels, attend_back(): pl.pallas_call(attend_back_kernel, grid_spec=pltpu.PrefetchScalarGridSpec...  43.7 us
    pallas_call x2, Pallas kernels, attend(): pl.pallas_call(attend_kernel, grid_spec=pltpu.PrefetchScalarGridSpec(num_...  30.7 us
    pallas_call x2, Pallas kernels, feed(): pl.pallas_call(feed_kernel, grid=(FF // width,), in_specs=[whole((rows, D...  29.4 us
    reduce_scatter x1, waiting for transfers between devices, plain_reduce(): lax.psum_scatter(square, BOTH, scatter_dimension=0, tiled=True).astype(F32)  28.1 us
  transfers between devices with their start and end apart: 12, of which 7 were waited for; matrix products, arithmetic and copies ran while one was open for 5% of the time, Pallas kernels for 62%

profile of v2, /device:TPU:0, one launch (start us, length us, event | category | flops | bytes accessed | tf_op | source)
XLA Modules:
  0.0 569.2 jit_solution(719059647639706941)
XLA Ops:
  12.1 92.6 %gather_0.1 = (bf16[768,6144]{1,0:T(8,128)(2,1)}, bf16[3072,768]{1,0:T(8,128)(2,1)S(1)}, bf16[768,256]{1,0:T(8,128)(2,1)S(1)}) custom-call(f32[1,24,256]{2,1,0:T(8,128)S(1)} %reshape.303.refs_0_, f32[2,24,2304]{2,1,0:T(8,128)S(1)} %copy-done.3, f32[2,24,768]{2,1,0:T(8,128)S(1)} %copy-done.4, f32[2,24,3072]{2,1,0:T(8,128)S(1)} %copy-done.2, ...), custom_call_target="tpu_custom_call" | custom-call | bytes 200000000 | tf_op jit(solution)/shard_map/gather_0/pallas_call | solution.py:328
  104.7 2.2 copy-done
  112.5 9.8 %project.2 = (bf16[512,768]{1,0:T(8,128)(2,1)}, bf16[2,512,768]{2,1,0:T(8,128)(2,1)}, bf16[512,768]{1,0:T(8,128)(2,1)}) custom-call(bf16[512,768]{1,0:T(8,128)(2,1)} %x_ref.5, bf16[768,6144]{1,0:T(8,128)(2,1)} %get-tuple-element.82.w_ref.wo_ref.we_ref, f32[1,6912]{1,0:T(1,128)} %slice.101.bias_ref.bo_ref.be_ref.bs_ref, f32[4,768]{1,0:T(4,128)} %squeeze.77.mod_ref, ...), custom_call_target="tpu_custom_call" | custom-call | flops 1811939328 | bytes 8000000 | tf_op jit(solution)/shard_map/project/pallas_call | solution.py:696
  122.3 3.3 collective-permute-start
  133.1 15.4 %attend.2 = (bf16[512,768]{1,0:T(8,128)(2,1)}, f32[6,8,512]{2,1,0:T(8,128)}) custom-call(s32[2,4]{1,0:T(2,128)} %pad_add_fusion.bounds_ref, bf16[512,768]{1,0:T(8,128)(2,1)} %get-tuple-element.84.q_ref, bf16[2,512,768]{2,1,0:T(8,128)(2,1)} %collective-permute-done.low_ref, bf16[2,512,768]{2,1,0:T(8,128)(2,1)} %get-tuple-element.85.own_ref, ...), custom_call_target="tpu_custom_call" | custom-call | flops 5000000000 | bytes 8000000 | tf_op jit(solution)/shard_map/attend/pallas_call | solution.py:793
  148.4 14.6 %feed.2 = (f32[512,768]{1,0:T(8,128)}, bf16[512,768]{1,0:T(8,128)(2,1)}, bf16[512,3072]{1,0:T(8,128)(2,1)}, bf16[512,3072]{1,0:T(8,128)(2,1)}, f32[512,768]{1,0:T(8,128)}) custom-call(bf16[512,768]{1,0:T(8,128)(2,1)} %get-tuple-element.86.o_ref, bf16[512,768]{1,0:T(8,128)(2,1)} %x_ref.5, bf16[768,6144]{1,0:T(8,128)(2,1)} %get-tuple-element.82.w_ref.wo_ref.we_ref, ...), custom_call_target="tpu_custom_call" | custom-call | flops 5435817984 | bytes 24000000 | tf_op jit(solution)/shard_map/feed/pallas_call | solution.py:927
  163.1 10.1 %project.3 = (bf16[512,768]{1,0:T(8,128)(2,1)}, bf16[2,512,768]{2,1,0:T(8,128)(2,1)}, bf16[512,768]{1,0:T(8,128)(2,1)}) custom-call(f32[512,768]{1,0:T(8,128)} %get-tuple-element.88.x_ref, bf16[768,6144]{1,0:T(8,128)(2,1)} %all-gather.4.cloned.1.call-done.w_ref.wo_ref.we_ref, f32[1,6912]{1,0:T(1,128)} %slice.108.bias_ref.bo_ref.be_ref.bs_ref, ...), custom_call_target="tpu_custom_call" | custom-call | flops 1811939328 | bytes 8000000 | tf_op jit(solution)/shard_map/project/pallas_call | solution.py:696
  173.2 22.2 %collective-permute-start.2 = (bf16[2,512,768]{2,1,0:T(8,128)(2,1)}, bf16[2,512,768]{2,1,0:T(8,128)(2,1)S(1)}, u32[]{:S(2)}, u32[]{:S(2)}) collective-permute-start(bf16[2,512,768]{2,1,0:T(8,128)(2,1)} %get-tuple-element.90.own_ref), channel_id=1, source_target_pairs={{0,1},{1,2},{2,3},{4,5},{5,6},{6,7},{8,9},{9,10},{10,11},{12,13},{... | collective-permute-start | bytes 4718600 | tf_op jit(solution)/shard_map/ppermute | solution.py:601
  198.6 2.4 collective-permute-done.3.high_ref
  202.1 15.3 %attend.3 = (bf16[512,768]{1,0:T(8,128)(2,1)}, f32[6,8,512]{2,1,0:T(8,128)}) custom-call(s32[2,4]{1,0:T(2,128)} %pad_add_fusion.bounds_ref, bf16[512,768]{1,0:T(8,128)(2,1)} %get-tuple-element.89.q_ref, bf16[2,512,768]{2,1,0:T(8,128)(2,1)} %copy-done.35, bf16[2,512,768]{2,1,0:T(8,128)(2,1)} %get-tuple-element.90.own_ref, bf16[2,512,768]{2,1,0:T(8,128)(2,1)} %copy-done.36, ...), custom_call_target="tpu_custom_call" | custom-call | flops 5000000000 | bytes 8000000 | tf_op jit(solution)/shard_map/attend/pallas_call | solution.py:793
  217.4 14.8 %feed.3 = (f32[512,768]{1,0:T(8,128)}, bf16[512,768]{1,0:T(8,128)(2,1)}, bf16[512,3072]{1,0:T(8,128)(2,1)}, bf16[512,3072]{1,0:T(8,128)(2,1)}, f32[512,768]{1,0:T(8,128)}) custom-call(bf16[512,768]{1,0:T(8,128)(2,1)} %get-tuple-element.91.o_ref, f32[512,768]{1,0:T(8,128)} %get-tuple-element.88.x_ref, ...), custom_call_target="tpu_custom_call" | custom-call | flops 5435817984 | bytes 24000000 | tf_op jit(solution)/shard_map/feed/pallas_call | solution.py:927
  232.3 23.2 %feed_back.2 = (bf16[768,6144]{1,0:T(8,128)(2,1)}, bf16[3072,768]{1,0:T(8,128)(2,1)}, f32[512,768]{1,0:T(8,128)}, bf16[512,768]{1,0:T(8,128)(2,1)}, f32[1,3072]{1,0:T(1,128)}, /*index=5*/f32[4,768]{1,0:T(4,128)}) custom-call(bf16[512,768]{1,0:T(8,128)(2,1)} %g_ref.1, bf16[512,3072]{1,0:T(8,128)(2,1)} %get-tuple-element.93.z_ref, ...), custom_call_target="tpu_custom_call" | custom-call | flops 10871635968 | bytes 40000000 | tf_op jit(solution)/shard_map/feed_back/pallas_call | solution.py:1010
  257.5 21.7 %attend_back.2 = (bf16[512,768]{1,0:T(8,128)(2,1)}, bf16[2,512,768]{2,1,0:T(8,128)(2,1)}, f32[2,512,768]{2,1,0:T(8,128)}, bf16[2,512,768]{2,1,0:T(8,128)(2,1)}) custom-call(s32[2,4]{1,0:T(2,128)} %pad_add_fusion.bounds_ref, bf16[512,768]{1,0:T(8,128)(2,1)} %get-tuple-element.89.q_ref, bf16[512,768]{1,0:T(8,128)(2,1)} %get-tuple-element.97.g_ref, ...), custom_call_target="tpu_custom_call" | custom-call | flops 12000000000 | bytes 16000000 | tf_op jit(solution)/shard_map/attend_back/pallas_call | solution.py:868
  279.3 22.8 %collective-permute-start.4 = (bf16[2,512,768]{2,1,0:T(8,128)(2,1)}, bf16[2,512,768]{2,1,0:T(8,128)(2,1)S(1)}, u32[]{:S(2)}, u32[]{:S(2)}) collective-permute-start(bf16[2,512,768]{2,1,0:T(8,128)(2,1)} %get-tuple-element.101), channel_id=1, source_target_pairs={{0,1},{1,2},{2,3},{4,5},{5,6},{6,7},{8,9},{9,10},{10,11},{12,13},{... | collective-permute-start | bytes 4718600 | tf_op jit(solution)/shard_map/ppermute | solution.py:601
  305.2 4.7 collective-permute-done.5.above_ref
  311.1 13.9 %project_back.2 = (bf16[768,6144]{1,0:T(8,128)(2,1)}, f32[512,768]{1,0:T(8,128)}, f32[1,2304]{1,0:T(1,128)}, f32[2,768]{1,0:T(2,128)}) custom-call(bf16[512,768]{1,0:T(8,128)(2,1)} %get-tuple-element.99.dq_ref, f32[2,512,768]{2,1,0:T(8,128)} %get-tuple-element.100.own_ref, bf16[2,512,768]{2,1,0:T(8,128)(2,1)} %copy-done.7, ...), custom_call_target="tpu_custom_call", output_to_operand_aliasing={{0}: (11, {})} | custom-call | flops 3623878656 | bytes 20000000 | tf_op jit(solution)/shard_map/project_back/pallas_call | solution.py:1104
  325.1 23.5 %feed_back.3 = (bf16[768,6144]{1,0:T(8,128)(2,1)}, bf16[3072,768]{1,0:T(8,128)(2,1)}, f32[512,768]{1,0:T(8,128)}, bf16[512,768]{1,0:T(8,128)(2,1)}, f32[1,3072]{1,0:T(1,128)}, /*index=5*/f32[4,768]{1,0:T(4,128)}) custom-call(f32[512,768]{1,0:T(8,128)} %get-tuple-element.106.g_ref, bf16[512,3072]{1,0:T(8,128)(2,1)} %get-tuple-element.107.z_ref, ...), custom_call_target="tpu_custom_call" | custom-call | flops 10871635968 | bytes 40000000 | tf_op jit(solution)/shard_map/feed_back/pallas_call | solution.py:1010
  348.7 22.0 %attend_back.3 = (bf16[512,768]{1,0:T(8,128)(2,1)}, bf16[2,512,768]{2,1,0:T(8,128)(2,1)}, f32[2,512,768]{2,1,0:T(8,128)}, bf16[2,512,768]{2,1,0:T(8,128)(2,1)}) custom-call(s32[2,4]{1,0:T(2,128)} %pad_add_fusion.bounds_ref, bf16[512,768]{1,0:T(8,128)(2,1)} %get-tuple-element.84.q_ref, bf16[512,768]{1,0:T(8,128)(2,1)} %get-tuple-element.111.g_ref, ...), custom_call_target="tpu_custom_call" | custom-call | flops 12000000000 | bytes 16000000 | tf_op jit(solution)/shard_map/attend_back/pallas_call | solution.py:868
  370.7 25.5 %collective-permute-start.6 = (bf16[2,512,768]{2,1,0:T(8,128)(2,1)}, bf16[2,512,768]{2,1,0:T(8,128)(2,1)S(1)}, u32[]{:S(2)}, u32[]{:S(2)}) collective-permute-start(bf16[2,512,768]{2,1,0:T(8,128)(2,1)} %get-tuple-element.115), channel_id=1, source_target_pairs={{0,1},{1,2},{2,3},{4,5},{5,6},{6,7},{8,9},{9,10},{10,11},{12,13},{... | collective-permute-start | bytes 4718600 | tf_op jit(solution)/shard_map/ppermute | solution.py:601
  399.6 3.3 collective-permute-done.7.above_ref
  402.9 14.1 %project_back.3 = (bf16[768,6144]{1,0:T(8,128)(2,1)}, f32[512,768]{1,0:T(8,128)}, f32[1,2304]{1,0:T(1,128)}, f32[2,768]{1,0:T(2,128)}) custom-call(bf16[512,768]{1,0:T(8,128)(2,1)} %get-tuple-element.113.dq_ref, f32[2,512,768]{2,1,0:T(8,128)} %get-tuple-element.114.own_ref, bf16[2,512,768]{2,1,0:T(8,128)(2,1)} %copy-done.6, ...), custom_call_target="tpu_custom_call", output_to_operand_aliasing={{0}: (11, {})} | custom-call | flops 3623878656 | bytes 20000000 | tf_op jit(solution)/shard_map/project_back/pallas_call | solution.py:1104
  420.1 99.4 %scatter_0.1 = (f32[24,256]{1,0:T(8,128)}, f32[24,2304]{1,0:T(8,128)}, f32[24,768]{1,0:T(8,128)}, f32[24,3072]{1,0:T(8,128)}, f32[96,768]{1,0:T(8,128)}) custom-call(bf16[768,6144]{1,0:T(8,128)(2,1)} %get-tuple-element.121.refs_0_, bf16[3072,768]{1,0:T(8,128)(2,1)} %get-tuple-element.122.refs_1_, bf16[768,256]{1,0:T(8,128)(2,1)} %convert_element_type.81.refs_2_), custom_call_target="tpu_custom_call" | custom-call | bytes 200000000 | tf_op jit(solution)/shard_map/scatter_0/pallas_call | solution.py:564
  526.5 2.6 fusion.24
  529.1 28.1 %reduce-scatter.3.cloned.1.call-done = bf16[24,6144]{1,0:T(8,128)(2,1)} async-done(((bf16[768,6144]{1,0:T(8,128)(2,1)}), bf16[24,6144]{1,0:T(8,128)(2,1)}) %reduce-scatter.3.cloned.1.call-update) | async-done | bytes 294928 | tf_op jit(solution)/shard_map/reduce_scatter | solution.py:1195
  (198 shorter events, 45.8 us)
Async XLA Ops:
  7.3 155.8 %all-gather.4.cloned.1.call-start = ((), (), s32[]{:S(2)}) async-start(), calls=%async_computation.2 | async-start | bytes 9732096 | tf_op jit(solution)/shard_map/all_gather | solution.py:1168
  11.0 206.4 %all-gather.6.cloned.1.call-start = ((), (), s32[]{:S(2)}) async-start(), calls=%async_computation.5 | async-start | bytes 4866048 | tf_op jit(solution)/shard_map/all_gather | solution.py:1169
  11.8 513.8 %reduce-scatter.5.cloned.1.call-start = ((), (), s32[]{:S(2)}) async-start(), calls=%async_computation.4 | async-start | bytes 4866048 | tf_op jit(solution)/shard_map/reduce_scatter | solution.py:1196
  122.3 9.3 %collective-permute-start = (bf16[2,512,768]{2,1,0:T(8,128)(2,1)}, bf16[2,512,768]{2,1,0:T(8,128)(2,1)}, u32[]{:S(2)}, u32[]{:S(2)}) collective-permute-start(bf16[2,512,768]{2,1,0:T(8,128)(2,1)} %get-tuple-element.85.own_ref), channel_id=1, source_target_pairs={{0,1},{1,2},{2,3},{4,5},{5,6},{6,7},{8,9},{9,10},{10,11},{12,13},{... | collective-permute-start | bytes 4718600 | tf_op jit(solution)/shard_map/ppermute | solution.py:601
  125.6 6.0 %collective-permute-start.1 = (bf16[2,512,768]{2,1,0:T(8,128)(2,1)}, bf16[2,512,768]{2,1,0:T(8,128)(2,1)}, u32[]{:S(2)}, u32[]{:S(2)}) collective-permute-start(bf16[2,512,768]{2,1,0:T(8,128)(2,1)} %get-tuple-element.85.own_ref), channel_id=1, source_target_pairs={{1,0},{2,1},{3,2},{5,4},{6,5},{7,6},{9,8},{10,9},{11,10},{13,12},{... | collective-permute-start | bytes 4718600 | tf_op jit(solution)/shard_map/ppermute | solution.py:601
  173.2 25.3 %collective-permute-start.2 = (bf16[2,512,768]{2,1,0:T(8,128)(2,1)}, bf16[2,512,768]{2,1,0:T(8,128)(2,1)S(1)}, u32[]{:S(2)}, u32[]{:S(2)}) collective-permute-start(bf16[2,512,768]{2,1,0:T(8,128)(2,1)} %get-tuple-element.90.own_ref), channel_id=1, source_target_pairs={{0,1},{1,2},{2,3},{4,5},{5,6},{6,7},{8,9},{9,10},{10,11},{12,13},{... | collective-permute-start | bytes 4718600 | tf_op jit(solution)/shard_map/ppermute | solution.py:601
  195.4 5.5 collective-permute-start.3
  255.5 301.7 %reduce-scatter.3.cloned.1.call-start = ((), (), s32[]{:S(2)}) async-start(), calls=%async_computation.3 | async-start | bytes 9732096 | tf_op jit(solution)/shard_map/reduce_scatter | solution.py:1195
  279.3 25.9 %collective-permute-start.4 = (bf16[2,512,768]{2,1,0:T(8,128)(2,1)}, bf16[2,512,768]{2,1,0:T(8,128)(2,1)S(1)}, u32[]{:S(2)}, u32[]{:S(2)}) collective-permute-start(bf16[2,512,768]{2,1,0:T(8,128)(2,1)} %get-tuple-element.101), channel_id=1, source_target_pairs={{0,1},{1,2},{2,3},{4,5},{5,6},{6,7},{8,9},{9,10},{10,11},{12,13},{... | collective-permute-start | bytes 4718600 | tf_op jit(solution)/shard_map/ppermute | solution.py:601
  302.0 7.8 %collective-permute-start.5 = (bf16[2,512,768]{2,1,0:T(8,128)(2,1)}, bf16[2,512,768]{2,1,0:T(8,128)(2,1)S(1)}, u32[]{:S(2)}, u32[]{:S(2)}) collective-permute-start(bf16[2,512,768]{2,1,0:T(8,128)(2,1)} %get-tuple-element.102), channel_id=1, source_target_pairs={{1,0},{2,1},{3,2},{5,4},{6,5},{7,6},{9,8},{10,9},{11,10},{13,12},{... | collective-permute-start | bytes 4718600 | tf_op jit(solution)/shard_map/ppermute | solution.py:601
  348.6 49.0 %copy-start.22 = (f32[4,768]{1,0:T(4,128)S(1)}, f32[4,768]{1,0:T(4,128)}, u32[]{:S(2)}) copy-start(f32[4,768]{1,0:T(4,128)} %get-tuple-element.127) | copy-start | bytes 36868
  348.6 49.0 %copy-start.27 = (f32[1,3072]{1,0:T(1,128)S(1)}, f32[1,3072]{1,0:T(1,128)}, u32[]{:S(2)}) copy-start(f32[1,3072]{1,0:T(1,128)} %get-tuple-element.128) | copy-start | bytes 36868
  348.6 49.1 %copy-start.34 = (f32[2,768]{1,0:T(2,128)S(1)}, f32[2,768]{1,0:T(2,128)}, u32[]{:S(2)}) copy-start(f32[2,768]{1,0:T(2,128)} %get-tuple-element.130) | copy-start | bytes 18436
  348.6 49.3 %copy-start.31 = (f32[1,2304]{1,0:T(1,128)S(1)}, f32[1,2304]{1,0:T(1,128)}, u32[]{:S(2)}) copy-start(f32[1,2304]{1,0:T(1,128)} %get-tuple-element.126) | copy-start | bytes 27652
  348.6 49.3 %copy-start.23 = (f32[4,768]{1,0:T(4,128)S(1)}, f32[4,768]{1,0:T(4,128)}, u32[]{:S(2)}) copy-start(f32[4,768]{1,0:T(4,128)} %get-tuple-element.124) | copy-start | bytes 36868
  348.6 49.4 %copy-start.28 = (f32[1,3072]{1,0:T(1,128)S(1)}, f32[1,3072]{1,0:T(1,128)}, u32[]{:S(2)}) copy-start(f32[1,3072]{1,0:T(1,128)} %get-tuple-element.125) | copy-start | bytes 36868
  370.7 28.9 %collective-permute-start.6 = (bf16[2,512,768]{2,1,0:T(8,128)(2,1)}, bf16[2,512,768]{2,1,0:T(8,128)(2,1)S(1)}, u32[]{:S(2)}, u32[]{:S(2)}) collective-permute-start(bf16[2,512,768]{2,1,0:T(8,128)(2,1)} %get-tuple-element.115), channel_id=1, source_target_pairs={{0,1},{1,2},{2,3},{4,5},{5,6},{6,7},{8,9},{9,10},{10,11},{12,13},{... | collective-permute-start | bytes 4718600 | tf_op jit(solution)/shard_map/ppermute | solution.py:601
  396.1 6.7 %collective-permute-start.7 = (bf16[2,512,768]{2,1,0:T(8,128)(2,1)}, bf16[2,512,768]{2,1,0:T(8,128)(2,1)}, u32[]{:S(2)}, u32[]{:S(2)}) collective-permute-start(bf16[2,512,768]{2,1,0:T(8,128)(2,1)} %get-tuple-element.116), channel_id=1, source_target_pairs={{1,0},{2,1},{3,2},{5,4},{6,5},{7,6},{9,8},{10,9},{11,10},{13,12},{... | collective-permute-start | bytes 4718600 | tf_op jit(solution)/shard_map/ppermute | solution.py:601
  420.1 100.4 %copy-start.29 = (f32[2,9,24]{2,0,1:T(2,128)S(1)}, f32[2,9,24]{2,0,1:T(2,128)}, u32[]{:S(2)}) copy-start(f32[2,9,24]{2,0,1:T(2,128)} %param.43) | copy-start | bytes 5188
  420.1 100.4 %copy-start.30 = (f32[2,9,24]{2,0,1:T(2,128)S(1)}, f32[2,9,24]{2,0,1:T(2,128)}, u32[]{:S(2)}) copy-start(f32[2,9,24]{2,0,1:T(2,128)} %param.44) | copy-start | bytes 5188
  420.1 102.9 %copy-start.24 = (f32[2,20,96]{2,0,1:T(2,128)S(1)}, f32[2,20,96]{2,0,1:T(2,128)}, u32[]{:S(2)}) copy-start(f32[2,20,96]{2,0,1:T(2,128)} %param.46) | copy-start | bytes 46084
  420.1 102.9 %copy-start.25 = (f32[2,20,96]{2,0,1:T(2,128)S(1)}, f32[2,20,96]{2,0,1:T(2,128)}, u32[]{:S(2)}) copy-start(f32[2,20,96]{2,0,1:T(2,128)} %param.47) | copy-start | bytes 46084
  420.1 106.4 %copy-start.9 = (f32[2,96,768]{2,1,0:T(8,128)S(1)}, f32[2,96,768]{2,1,0:T(8,128)}, u32[]{:S(2)}) copy-start(f32[2,96,768]{2,1,0:T(8,128)} %param.40) | copy-start | bytes 1769476
  420.1 106.4 %copy-start.10 = (f32[2,96,768]{2,1,0:T(8,128)S(1)}, f32[2,96,768]{2,1,0:T(8,128)}, u32[]{:S(2)}) copy-start(f32[2,96,768]{2,1,0:T(8,128)} %param.41) | copy-start | bytes 1769476
  (25 other events, 175.4 us)
Sparse Core Ops, SparseCore 0:
  11.6 103.2 all-gather.3
  118.4 64.7 all-gather.5
  255.6 124.9 reduce-scatter.4
  387.4 169.7 reduce-scatter.2
